TPU v7x, 32 devices: a whole 2x2x4 slice. The times are simulated.
32 devices in a mesh: row: 4 (over z), ma: 8 (over y, x, core).
Axes of the slice: x: 2, y: 2, z: 4, core: 2. Of those that a mesh axis runs over, the one named last changes fastest.
Arguments:
- toroidal_stream_spectra: float32 [2, 4, 512, 512], P(None, 'row', 'ma'), may hold values from -6 to 6, as said below
- thermal_spectra: float32 [2, 4, 512, 512], P(None, 'row', 'ma'), may hold values from -6 to 6, as said below
- induction_potential: float32 [2, 4, 512, 512], P(None, 'row', 'ma'), may hold values from -6 to 6, as said below
- outward_speed_spectra: float32 [2, 4, 512, 512], P(None, 'row', 'ma'), may hold values from -60 to 60, as said below
- position_azimuth_map: int32 [512], replicated, may hold values from 0 to 511, as said below
- subdiagonal_complement: float32 [2, 4, 512], P(None, 'row'), may hold values from 0.005 to 0.3
- superdiagonal_complement: float32 [2, 4, 512], P(None, 'row'), may hold values from 0.005 to 0.3
- diagonal_entries: float32 [2, 4, 512], P(None, 'row'), may hold values from 2 to 16
Outputs:
- new_temperature: float32 [2, 4, 512, 512], P(None, 'row', 'ma')
- new_magnetic: float32 [2, 4, 512, 512], P(None, 'row', 'ma')
Inputs may be any that keep to these rules, and one draw needn't show every extreme that they name: `position_azimuth_map`: slots 2 i and 2 i + 1 hold the orders m and 511 - m; every order stands in exactly one slot. `toroidal_stream_spectra`: an entry whose degree is below the order of its slot in position_azimuth_map is zero. `thermal_spectra`: an entry whose degree is below the order of its slot in position_azimuth_map is zero. `induction_potential`: an entry whose degree is below the order of its slot in position_azimuth_map is zero. `outward_speed_spectra`: an entry whose degree is below the order of its slot in position_azimuth_map is zero.
All inputs are finite; a program needn't handle non-finite values.
Results may differ from a plain program's by a relative error of at most 0.00035.
Values sent between devices are 32-bit elements; how exact they have to be, the bound alone decides.
A program may use at most 128 MiB of HBM per device.

v0:
```python
import math

import jax
import jax.numpy as jnp
from jax import lax
from jax.sharding import PartitionSpec as P

NLAT = 768
NLON = 1536


inner_radius = 0.35
shell_span = 0.65
time_step = 0.001
highest = lax.Precision.HIGHEST
log_gamma_half = 0.5 * math.log(math.pi) - math.log(2.0)


def extended(block, sides, width):
    for axis, dim in sides:
        count = lax.axis_size(axis)
        forward = [(i, i + 1) for i in range(count - 1)]
        backward = [(target, source) for source, target in forward]
        low = lax.ppermute(
            lax.slice_in_dim(block, block.shape[dim] - width, None, axis=dim), axis, forward
        )
        high = lax.ppermute(lax.slice_in_dim(block, 0, width, axis=dim), axis, backward)
        block = jnp.concatenate([low, block, high], axis=dim)
    return block


def entering_2(part, axis, combine, identity, reverse):
    count = lax.axis_size(axis)
    place = lax.axis_index(axis)
    ahead = count - 1 - place if reverse else place
    gathered = jax.tree.map(lambda a: lax.all_gather(a, axis), part)
    state = jax.tree.map(lambda a, e: jnp.zeros_like(a) + jnp.asarray(e, a.dtype), part, identity)

    def one(step, state):
        source = count - 1 - step if reverse else step
        return combine(
            state, jax.tree.map(lambda a: lax.dynamic_index_in_dim(a, source, 0, False), gathered)
        )

    return lax.fori_loop(0, ahead, one, state)


def legendre_rows(orders, cosine, sine_vals, harmonic_index_array):
    block_len = math.gcd(32, harmonic_index_array)
    dtype_ref = cosine.dtype
    order_col = orders[:, None]
    log_start = (
        0.5 * (lax.lgamma(order_col + 1.5) - lax.lgamma(order_col + 1.0) - log_gamma_half)
        - 0.5 * math.log(2.0)
        + order_col * jnp.log(sine_vals)[None, :]
    )
    zero_state = jnp.zeros(log_start.shape, dtype_ref)
    legendre = jnp.zeros((orders.shape[0], harmonic_index_array, cosine.shape[0]), dtype_ref)

    def sweep(position, state_tuple):
        before, current, log_scale, legendre = state_tuple
        new_rows = []
        for offset in range(block_len):
            degree_now = (position * block_len + offset).astype(dtype_ref)
            above_diag = degree_now > order_col
            square = degree_now * degree_now - order_col * order_col
            denominator = jnp.where(above_diag, square, 1.0)
            rise_coef = jnp.where(
                above_diag,
                jnp.sqrt(jnp.maximum(4.0 * degree_now * degree_now - 1.0, 1.0) / denominator),
                0.0,
            )
            lower_term = (degree_now - 1.0) * (degree_now - 1.0) - order_col * order_col
            fall_coef = jnp.where(
                above_diag,
                jnp.sqrt(
                    jnp.maximum((2.0 * degree_now + 1.0) * lower_term, 0.0)
                    / (jnp.maximum(2.0 * degree_now - 3.0, 1.0) * denominator)
                ),
                0.0,
            )
            fresh_row = jnp.where(
                degree_now == order_col,
                1.0,
                rise_coef * cosine[None, :] * current - fall_coef * before,
            )
            before, current = (current, fresh_row)
            new_rows.append(fresh_row * jnp.exp(log_scale))
        magnitude = jnp.maximum(jnp.abs(before), jnp.abs(current))
        magnitude = jnp.where(magnitude > 0.0, magnitude, 1.0)
        before = before / magnitude
        current = current / magnitude
        log_scale = log_scale + jnp.log(magnitude)
        first_row = (position * block_len).astype(jnp.int32)
        legendre = lax.dynamic_update_slice(
            legendre, jnp.stack(new_rows, axis=1), (jnp.int32(0), first_row, jnp.int32(0))
        )
        return (before, current, log_scale, legendre)

    state_tuple = lax.fori_loop(
        0, harmonic_index_array // block_len, sweep, (zero_state, zero_state, log_start, legendre)
    )
    return state_tuple[3]


def wave_table(orders, first_col, column_count, lon_total):
    column_ids = first_col + jnp.arange(column_count, dtype=jnp.int32)
    phase_int = orders[:, None] * column_ids[None, :] % lon_total
    angle_vals = 2.0 * math.pi / lon_total * phase_int.astype(jnp.float32)
    return jnp.stack([jnp.cos(angle_vals), -jnp.sin(angle_vals)], axis=1)


def to_longitudes(spectra, orders, lon_total):
    order_weight = jnp.where(orders == 0, 1.0, 2.0).astype(spectra.dtype)
    weighted = spectra * order_weight[:, None, None, None, None]
    lon_block = math.gcd(512, lon_total)
    output_buf = jnp.zeros(
        (spectra.shape[1], spectra.shape[2], spectra.shape[4], lon_total), spectra.dtype
    )

    def place(position, output_buf):
        first_col = (position * lon_block).astype(jnp.int32)
        wave_block = wave_table(orders, first_col, lon_block, lon_total)
        grid_piece = jnp.einsum("mfscn,mcp->fsnp", weighted, wave_block, precision=highest)
        return lax.dynamic_update_slice(
            output_buf, grid_piece, (jnp.int32(0), jnp.int32(0), jnp.int32(0), first_col)
        )

    return lax.fori_loop(0, lon_total // lon_block, place, output_buf)


def from_longitudes(grid_sets, orders, lon_total):
    lon_block = math.gcd(512, lon_total)
    running_sum = jnp.zeros(
        (orders.shape[0], grid_sets.shape[0], grid_sets.shape[1], 2, grid_sets.shape[2]),
        grid_sets.dtype,
    )

    def add_block(position, running_sum):
        first_col = (position * lon_block).astype(jnp.int32)
        wave_block = wave_table(orders, first_col, lon_block, lon_total)
        grid_piece = lax.dynamic_slice_in_dim(grid_sets, first_col, lon_block, 3)
        return running_sum + jnp.einsum(
            "fsnp,mcp->mfscn", grid_piece, wave_block, precision=highest
        )

    return lax.fori_loop(0, lon_total // lon_block, add_block, running_sum) / lon_total


def fejer_weights(node_count, lat_total):
    term_count = lat_total // 2
    wave_ints = jnp.arange(1, term_count + 1, dtype=jnp.int32)
    node_ints = 2 * jnp.arange(node_count, dtype=jnp.int32) + 1
    phase_int = wave_ints[:, None] * node_ints[None, :] % (2 * lat_total)
    cosines = jnp.cos(math.pi / lat_total * phase_int.astype(jnp.float32))
    wave_vals = wave_ints.astype(jnp.float32)
    ratio_vals = cosines / (4.0 * wave_vals * wave_vals - 1.0)[:, None]
    return 2.0 / lat_total * (1.0 - 2.0 * jnp.sum(ratio_vals, axis=0))


def nonlinear(grid_sets, factor):
    heat_term = -(
        (grid_sets[3] * grid_sets[1] - grid_sets[0] * grid_sets[4]) * factor
        + grid_sets[6] * grid_sets[7]
    )
    field_term = -(
        (grid_sets[3] * grid_sets[2] - grid_sets[0] * grid_sets[5]) * factor
        + grid_sets[6] * grid_sets[8]
    )
    return jnp.stack([heat_term, field_term])


def join_maps(earlier_map, later_map):
    return (
        earlier_map[0] * later_map[0],
        earlier_map[1] * later_map[0][:, None, None, :] + later_map[1],
    )


def body(
    toroidal_stream_spectra,
    thermal_spectra,
    induction_potential,
    outward_speed_spectra,
    position_azimuth_map,
    subdiagonal_complement,
    superdiagonal_complement,
    diagonal_entries,
):
    layer_indices = thermal_spectra.shape[1]
    local_azimuthal_numbers = thermal_spectra.shape[2]
    harmonic_index_array = thermal_spectra.shape[3]
    latitude_rows = NLAT // lax.axis_size("ma")
    north_count = NLAT // 2
    spacing = shell_span / (layer_indices * lax.axis_size("row"))
    slot_start = lax.axis_index("ma") * local_azimuthal_numbers
    my_orders = lax.dynamic_slice_in_dim(position_azimuth_map, slot_start, local_azimuthal_numbers)
    order_float = my_orders.astype(jnp.float32)
    degree_vals = jnp.arange(harmonic_index_array, dtype=jnp.float32)
    degree_ints = jnp.arange(harmonic_index_array, dtype=jnp.int32)
    even_mask = (my_orders[:, None] + degree_ints[None, :]) % 2 == 0
    parity_sign = jnp.where(even_mask, 1.0, -1.0)
    above_diag = degree_vals[None, :] > order_float[:, None]
    link_coef = jnp.where(
        above_diag,
        jnp.sqrt(
            jnp.maximum(
                (2.0 * degree_vals + 1.0)
                * (degree_vals * degree_vals - order_float[:, None] * order_float[:, None]),
                0.0,
            )
            / jnp.maximum(2.0 * degree_vals - 1.0, 1.0)
        ),
        0.0,
    )
    theta_all = math.pi * (jnp.arange(NLAT, dtype=jnp.float32) + 0.5) / NLAT
    cosine_all = jnp.cos(theta_all)
    cosine_north = cosine_all[:north_count]
    sine_north = jnp.sin(theta_all[:north_count])
    weights = fejer_weights(north_count, NLAT)
    legendre_all = legendre_rows(order_float, cosine_north, sine_north, harmonic_index_array)
    coupled_quantities = jnp.stack([thermal_spectra, induction_potential])
    motion_groupings = jnp.stack([toroidal_stream_spectra, thermal_spectra, induction_potential])
    weighted = motion_groupings * degree_vals
    product = motion_groupings * link_coef[None, None, None]
    lifted = jnp.concatenate([product[..., 1:], jnp.zeros_like(product[..., :1])], axis=-1)
    coef_sets = jnp.concatenate(
        [motion_groupings, weighted, lifted, outward_speed_spectra[None]], axis=0
    )
    set_count = 10
    coeffs = jnp.transpose(coef_sets, (3, 0, 2, 1, 4)).reshape(
        local_azimuthal_numbers, set_count * layer_indices * 2, harmonic_index_array
    )
    column_count = coeffs.shape[1]
    stacked = jnp.concatenate([coeffs, coeffs * parity_sign[:, None, :]], axis=1)
    result = jnp.einsum("ocl,oln->ocn", stacked, legendre_all, precision=highest)
    result = jnp.concatenate(
        [result[:, :column_count], jnp.flip(result[:, column_count:], axis=2)], axis=2
    ).reshape(local_azimuthal_numbers, set_count, layer_indices, 2, NLAT)
    plain_part = result[:, 0:3]
    slant_part = cosine_all * result[:, 3:6] - result[:, 6:9]
    outgoing = jnp.concatenate([plain_part, slant_part, result[:, 9:10]], axis=1)
    arrived = lax.all_to_all(outgoing, "ma", split_axis=4, concat_axis=0, tiled=True)
    spin_all = position_azimuth_map.astype(jnp.float32)[:, None, None, None]
    base_part = arrived[:, 0:3]
    turned_all = jnp.stack(
        [-spin_all * base_part[:, :, :, 1], spin_all * base_part[:, :, :, 0]], axis=3
    )
    full_sets = jnp.concatenate([turned_all, arrived[:, 3:7], base_part[:, 1:3]], axis=1)
    grid_sets = to_longitudes(full_sets, position_azimuth_map, NLON)
    padded = extended(grid_sets[7:9], (("row", 1),), 1)
    depthwise_slope = (padded[:, 2:] - padded[:, :-2]) / (2.0 * spacing)
    grid_sets = jnp.concatenate([grid_sets[0:7], depthwise_slope], axis=0)
    lat_index = lax.axis_index("ma") * latitude_rows + jnp.arange(latitude_rows, dtype=jnp.int32)
    theta_mine = math.pi * (lat_index.astype(jnp.float32) + 0.5) / NLAT
    sine_mine = jnp.sin(theta_mine)
    shell_index = lax.axis_index("row") * layer_indices + jnp.arange(layer_indices, dtype=jnp.int32)
    radius = inner_radius + spacing * (shell_index.astype(jnp.float32) + 0.5)
    factor = 1.0 / (radius[:, None] * radius[:, None] * (sine_mine * sine_mine)[None, :])
    forcing = nonlinear(grid_sets, factor[:, :, None])
    spectra = from_longitudes(forcing, position_azimuth_map, NLON)
    returned = lax.all_to_all(spectra, "ma", split_axis=0, concat_axis=4, tiled=True)
    values = returned.reshape(local_azimuthal_numbers, 4 * layer_indices, NLAT)
    column_count = values.shape[1]
    north_part = values[:, :, :north_count]
    south_part = jnp.flip(values[:, :, north_count:], axis=2)
    stacked = jnp.concatenate(
        [(north_part + south_part) * weights, (north_part - south_part) * weights], axis=1
    )
    result = jnp.einsum("ocn,oln->ocl", stacked, legendre_all, precision=highest)
    tendency = jnp.where(even_mask[:, None, :], result[:, :column_count], result[:, column_count:])
    tendency = jnp.transpose(
        tendency.reshape(local_azimuthal_numbers, 2, layer_indices, 2, harmonic_index_array),
        (1, 3, 2, 0, 4),
    )
    right_side = coupled_quantities + time_step * tendency
    keep_low = 1.0 - subdiagonal_complement
    keep_up = 1.0 - superdiagonal_complement
    unit_gains = jnp.ones((2, harmonic_index_array), jnp.float32)
    zero_block = jnp.zeros(right_side[:, :, 0].shape, jnp.float32)
    running_sum = zero_block
    through = unit_gains
    each_shell = 0
    running_sum = (
        right_side[:, :, each_shell] + keep_low[:, each_shell][:, None, None, :] * running_sum
    )
    through = through * keep_low[:, each_shell]
    entering = entering_2(
        (through, running_sum), "row", join_maps, (unit_gains, zero_block), False
    )[1]
    running = entering
    each_shell = 0
    running = right_side[:, :, each_shell] + keep_low[:, each_shell][:, None, None, :] * running
    scaled = [running / diagonal_entries[:, each_shell][:, None, None, :]]
    running_sum = zero_block
    through = unit_gains
    for each_shell in reversed(range(layer_indices)):
        running_sum = scaled[each_shell] + keep_up[:, each_shell][:, None, None, :] * running_sum
        through = through * keep_up[:, each_shell]
    entering = entering_2((through, running_sum), "row", join_maps, (unit_gains, zero_block), True)[
        1
    ]
    running = entering
    results = []
    for each_shell in reversed(range(layer_indices)):
        running = scaled[each_shell] + keep_up[:, each_shell][:, None, None, :] * running
        results.append(running)
    solved = jnp.stack(results[::-1], axis=2)
    return (solved[0], solved[1])


def solution(mesh):
    in_specs = (
        P(None, "row", "ma", None),
        P(None, "row", "ma", None),
        P(None, "row", "ma", None),
        P(None, "row", "ma", None),
        P(),
        P(None, "row", None),
        P(None, "row", None),
        P(None, "row", None),
    )
    out_specs = (P(None, "row", "ma", None), P(None, "row", "ma", None))
    return jax.shard_map(body, mesh=mesh, in_specs=in_specs, out_specs=out_specs, check_vma=False)
```

profile of v0, /device:TPU:2, one launch (start us, length us, event | category | flops | bytes accessed | tf_op | source)
XLA Modules:
  0.0 1020.6 jit_solution(8351865329401318251)
XLA Ops:
  11.1 16.5 %broadcast_in_dim.921.clone = f32[64,512,384]{2,1,0:T(8,128)} broadcast(f32[]{:T(128)} %constant.782.clone.1), dimensions={} | broadcast | bytes 50331652 | tf_op jit(solution)/shard_map/broadcast_in_dim | solution.py:58
  27.6 564.5 %while.85 = (s32[]{:T(128)}, f32[64,384]{1,0:T(8,128)S(1)}, f32[64,384]{1,0:T(8,128)S(1)}, f32[64,384]{1,0:T(8,128)S(1)}, f32[64,512,384]{2,1,0:T(8,128)}, /*ind...) while((s32[]{:T(128)}, f32[64,384]{1,0:T(8,128)S(1)}, ...), condition=%wide.region_1.2_spmd.clone.clone, body=%wide.region_0.1_spmd.clone.clone.sunk | while | flops 8507365 | bytes 22588916 | solution.py:100
  601.1 32.8 %fusion.32 = f32[64,40,384]{2,1,0:T(8,128)S(1)} fusion(f32[64,512,384]{2,1,0:T(8,128)} %get-tuple-element.812, f32[64,20,512]{2,1,0:T(8,128)} %get-tuple-element.1141, f32[64,20,512]{2,1,0:T(8,128)S(1)} %get-tuple-element.1140), kind=kOutput, calls=%fused_computation.272 | convolution fusion | flops 6041108480 | bytes 59506688 | tf_op jit(solution)/shard_map/ocl,oln->ocn/dot_general | solution.py:236
  644.4 7.8 copy.70
  652.1 9.3 reshape.2896
  661.5 4.8 all-to-all-start
  666.3 31.7 %all-to-all-done = f32[8,1,86016]{2,1,0:T(1,128)S(1)} async-done(((f32[8,1,86016]{2,1,0:T(1,128)}), f32[8,1,86016]{2,1,0:T(1,128)S(1)}, u32[]{:S(2)}, u32[]{:S(2)}) %all-to-all-start) | async-done | bytes 2752544 | tf_op jit(solution)/shard_map/all_to_all | solution.py:243
  698.5 10.0 reduce.2
  708.5 8.3 reshape.2897
  716.8 9.5 copy.71
  733.4 5.6 copy.72
  742.0 38.6 %while.81 = (s32[]{:T(128)}, f32[9,1,96,1536]{3,2,0,1:T(8,128)}, s32[512]{0:T(512)S(1)}, f32[512,9,1,2,96]{0,4,3,1,2:T(8,128)}, s32[]{:T(128)}, /*index=5*/s32[]{:T(128)}, s32[]{:T(128)}, s32[]{:T(128)}) while((s32[]{:T(128)}, f32[9,1,96,1536]{3,2,0,1:T(8,128)}, s32[512]{0:T(512)S(1)}, f32[512,9,1,2,96]{0,4,3,1,2:T(8,128)}, s32[]{:T(128)}, ...), condition=%wide.region_3.4_spmd, body=%wide.region_2.3_spmd.sunk | while | flops 5438964224 | bytes 9509011 | solution.py:129
  746.4 8.5 bitcast_dynamic-update-slice_fusion.67
  759.2 8.5 bitcast_dynamic-update-slice_fusion.67
  772.1 8.6 bitcast_dynamic-update-slice_fusion.67
  784.3 5.6 collective-permute-start.1
  792.9 20.2 %collective-permute-done = f32[2,1,96,1536]{3,2,0,1:T(8,128)S(1)} collective-permute-done((f32[2,1,96,1536]{3,2,0,1:T(8,128)}, f32[2,1,96,1536]{3,2,0,1:T(8,128)S(1)}, u32[]{:S(2)}, u32[]{:S(2)}) %collective-permute-start) | collective-permute-done | bytes 1179680 | tf_op jit(solution)/shard_map/ppermute | solution.py:27
  819.6 23.6 %while.84 = (s32[]{:T(128)}, f32[512,2,1,2,96]{0,4,1,3,2:T(8,128)S(1)}, s32[512]{0:T(512)S(1)}, f32[2,1,96,1536]{3,2,0,1:T(8,128)}, s32[]{:T(128)}, /*index=5*/s32[]{:T(128)}, s32[]{:T(128)}, s32[]{:T(128)}) while((s32[]{:T(128)}, f32[512,2,1,2,96]{0,4,1,3,2:T(8,128)S(1)}, s32[512]{0:T(512)S(1)}, f32[2,1,96,1536]{3,2,0,1:T(8,128)}, ...), condition=%wide.region_5.6_spmd.clone, body=%wide.region_4.5_spmd.clone.sunk | while | flops 1211499008 | bytes 6166685 | solution.py:147
  848.4 13.4 %all-to-all-done.1 = f32[512,2,1,2,96]{4,3,1,2,0:T(2,128)S(1)} async-done(((f32[512,2,1,2,96]{4,3,1,2,0:T(2,128)}), f32[512,2,1,2,96]{4,3,1,2,0:T(2,128)S(1)}, u32[]{:S(2)}, u32[]{:S(2)}) %all-to-all-start.1) | async-done | bytes 786464 | tf_op jit(solution)/shard_map/all_to_all | solution.py:262
  864.2 45.5 %fusion.36 = f32[64,8,512]{2,1,0:T(8,128)S(1)} fusion(f32[64,512,384]{2,1,0:T(8,128)} %get-tuple-element.812, f32[64,4,384]{2,1,0:T(4,128)S(1)} %get-tuple-element.1143, f32[64,4,384]{2,1,0:T(4,128)S(1)} %get-tuple-element.1142), kind=kOutput, calls=%fused_computation.289 | convolution fusion | flops 1208156160 | bytes 52166656 | tf_op jit(solution)/shard_map/ocn,oln->ocl/dot_general | solution.py:270
  911.2 14.3 %all-gather = f32[8,1,512]{2,1,0:T(1,128)S(1)} all-gather(f32[2,1,512]{2,1,0:T(1,128)S(1)} %broadcast_subtract_fusion), channel_id=2, replica_groups=mesh['row'=4,'ma'=8] {'row'}, dimensions={0}, use_global_device_ids=true | all-gather | bytes 20480 | tf_op jit(solution)/shard_map/all_gather | solution.py:36
  925.6 33.1 %all-gather.6.cloned.1.call-done = f32[4,2,2,64,512]{4,3,2,1,0:T(8,128)} async-done(((f32[1,2,2,64,512]{4,3,2,1,0:T(8,128)}), f32[4,2,2,64,512]{4,3,2,1,0:T(8,128)}) %all-gather.6.cloned.1.call-update) | async-done | bytes 2097168 | tf_op jit(solution)/shard_map/all_gather | solution.py:36
  959.8 14.3 %all-gather.1 = f32[8,1,512]{2,1,0:T(1,128)S(1)} all-gather(f32[2,1,512]{2,1,0:T(1,128)S(1)} %copy.81), channel_id=3, replica_groups=mesh['row'=4,'ma'=8] {'row'}, dimensions={0}, use_global_device_ids=true | all-gather | bytes 20480 | tf_op jit(solution)/shard_map/all_gather | solution.py:36
  974.2 34.2 %all-gather.8.cloned.1.call-done = f32[8,2,64,512]{3,2,1,0:T(8,128)} async-done(((f32[2,2,64,512]{3,2,1,0:T(8,128)}), f32[8,2,64,512]{3,2,1,0:T(8,128)}) %all-gather.8.cloned.1.call-update) | async-done | bytes 2097168 | tf_op jit(solution)/shard_map/all_gather | solution.py:36
  (1538 shorter events, 652.5 us)
Async XLA Ops:
  45.1 10.1 copy-start.9
  80.4 10.1 copy-start.9
  115.7 10.1 copy-start.9
  151.0 10.1 copy-start.9
  186.3 10.1 copy-start.9
  221.6 10.1 copy-start.9
  256.8 10.1 copy-start.9
  292.0 10.1 copy-start.9
  327.3 10.1 copy-start.9
  362.6 10.1 copy-start.9
  397.9 10.1 copy-start.9
  433.2 10.1 copy-start.9
  468.5 10.1 copy-start.9
  503.7 10.1 copy-start.9
  538.9 10.1 copy-start.9
  661.5 36.5 %all-to-all-start = ((f32[8,1,86016]{2,1,0:T(1,128)}), f32[8,1,86016]{2,1,0:T(1,128)S(1)}, u32[]{:S(2)}, u32[]{:S(2)}) async-start(f32[8,1,86016]{2,1,0:T(1,128)} %reshape.2896), calls=%async_computation | async-start | bytes 5505024 | tf_op jit(solution)/shard_map/all_to_all | solution.py:243
  783.0 30.0 %collective-permute-start = (f32[2,1,96,1536]{3,2,0,1:T(8,128)}, f32[2,1,96,1536]{3,2,0,1:T(8,128)S(1)}, u32[]{:S(2)}, u32[]{:S(2)}) collective-permute-start(f32[2,1,96,1536]{3,2,0,1:T(8,128)} %slice.184), channel_id=1, source_target_pairs={{8,0},{16,8},{24,16},{9,1},{17,9},{25,17},{10,2},{18,10},{26,18},{... | collective-permute-start | bytes 3538952 | tf_op jit(solution)/shard_map/ppermute | solution.py:27
  784.3 30.0 %collective-permute-start.1 = (f32[2,1,96,1536]{3,2,0,1:T(8,128)}, f32[2,1,96,1536]{3,2,0,1:T(8,128)}, u32[]{:S(2)}, u32[]{:S(2)}) collective-permute-start(f32[2,1,96,1536]{3,2,0,1:T(8,128)} %slice.184), channel_id=1, source_target_pairs={{0,8},{8,16},{16,24},{1,9},{9,17},{17,25},{2,10},{10,18},{18,26},{... | collective-permute-start | bytes 3538952 | tf_op jit(solution)/shard_map/ppermute | solution.py:24
  844.6 17.2 %all-to-all-start.1 = ((f32[512,2,1,2,96]{4,3,1,2,0:T(2,128)}), f32[512,2,1,2,96]{4,3,1,2,0:T(2,128)S(1)}, u32[]{:S(2)}, u32[]{:S(2)}) async-start(f32[512,2,1,2,96]{4,3,1,2,0:T(2,128)} %copy.74), calls=%async_computation.1 | async-start | bytes 2097152 | tf_op jit(solution)/shard_map/all_to_all | solution.py:262
  848.1 110.6 %all-gather.6.cloned.1.call-start = ((), (), s32[]{:S(2)}) async-start(), calls=%async_computation.2 | async-start | bytes 2621440 | tf_op jit(solution)/shard_map/all_gather | solution.py:36
  864.2 46.0 %copy-start = (f32[2,1,64,512]{3,2,1,0:T(8,128)S(1)}, f32[2,1,64,512]{3,2,1,0:T(8,128)}, u32[]{:S(2)}) copy-start(f32[2,1,64,512]{3,2,1,0:T(8,128)} %param.20) | copy-start | bytes 786436
  864.2 46.0 %copy-start.1 = (f32[2,1,64,512]{3,2,1,0:T(8,128)S(1)}, f32[2,1,64,512]{3,2,1,0:T(8,128)}, u32[]{:S(2)}) copy-start(f32[2,1,64,512]{3,2,1,0:T(8,128)} %param.19) | copy-start | bytes 786436
  909.7 15.9 %copy-start.25 = (f32[2,1,512]{2,1,0:T(1,128)S(1)}, f32[2,1,512]{2,1,0:T(1,128)}, u32[]{:S(2)}) copy-start(f32[2,1,512]{2,1,0:T(1,128)} %param.24) | copy-start | bytes 12292
  911.1 97.3 %all-gather.8.cloned.1.call-start = ((), (), s32[]{:S(2)}) async-start(), calls=%async_computation.3 | async-start | bytes 2621440 | tf_op jit(solution)/shard_map/all_gather | solution.py:36
  (298 other events, 1309.2 us)
Sparse Core Ops, SparseCore 0:
  911.2 47.4 all-gather.5
  960.3 48.0 all-gather.7
where the time goes:
time: 1040 us; the launch traced here: 1020 us
  other arithmetic  560 us (54%)
  local copies, waits for them, and re-layouts  139 us (13%)
  waiting for transfers between devices  134 us (13%)
  matrix products  114 us (11%)
  blocking collectives  28.6 us (3%)
  starting transfers between devices  15.3 us (1%)
  between operations  15.1 us (1%)
  loops' own time  14.3 us (1%)
    while x496, other arithmetic  360 us
    select_n x176, other arithmetic, sweep(): jnp.where(above_diag, jnp.sqrt(jnp.maximum(4.0 * degree_now * degree_now...  80.2 us
    all_gather x2, waiting for transfers between devices, entering_2(): gathered = jax.tree.map(lambda a: lax.all_gather(a, axis), part)  67.3 us
    dynamic_update_slice x16, local copies, waits for them, and re-layouts, sweep(): lax.dynamic_update_slice(legendre, jnp.stack(new_rows, axis=1), (jnp.int3...  56.3 us
    dot_general x1, matrix products, body(): jnp.einsum('ocn,oln->ocl', stacked, legendre_all, precision=highest)  45.5 us
    dot_general x1, matrix products, body(): jnp.einsum('ocl,oln->ocn', stacked, legendre_all, precision=highest)  32.8 us
    all_to_all x1, waiting for transfers between devices, body(): lax.all_to_all(outgoing, 'ma', split_axis=4, concat_axis=0, tiled=True)  31.7 us
    all_gather x2, blocking collectives, entering_2(): gathered = jax.tree.map(lambda a: lax.all_gather(a, axis), part)  28.6 us
  transfers between devices with their start and end apart: 6, of which 6 were waited for; matrix products, arithmetic and copies ran while one was open for 0% of the time, Pallas kernels for 0%

commit v1 on v0

--- a/solution.py
+++ b/solution.py
@@ -1,8 +1,11 @@
+import functools
 import math
 
 import jax
 import jax.numpy as jnp
 from jax import lax
+from jax.experimental import pallas as pl
+from jax.experimental.pallas import tpu as pltpu
 from jax.sharding import PartitionSpec as P
 
 NLAT = 768
@@ -309,6 +312,516 @@
     return (solved[0], solved[1])
 
 
+VMEM_BYTES = 60 * 1024 * 1024
+SET_ROWS = 48
+PROFILE_ROWS = 32
+
+
+def halves(values):
+    high = values.astype(jnp.bfloat16)
+    return high, (values - high.astype(jnp.float32)).astype(jnp.bfloat16)
+
+
+def dot(left, right):
+    return jnp.dot(left, right, preferred_element_type=jnp.float32)
+
+
+def dot_t(left, right):
+    return lax.dot_general(
+        left, right, (((1,), (1,)), ((), ())), preferred_element_type=jnp.float32
+    )
+
+
+def synthesis_kernel(
+    psi_ref, heat_ref, mag_ref, speed_ref, link_ref, sign_ref, rise_ref, fall_ref, diag_ref,
+    log_ref, cos_ref, out_ref, high_ref, low_ref, table, coef, prof, *, step_count,
+):
+    step = pl.program_id(0)
+    group, degrees = link_ref.shape
+    north = cos_ref.shape[1]
+    local = group * step_count
+    targets, quantities, rows, lanes = out_ref.shape
+    half = rows // 2
+
+    @pl.when(step == 0)
+    def _():
+        coef[...] = jnp.zeros_like(coef)
+
+    degree = lax.broadcasted_iota(jnp.int32, (group, degrees), 1).astype(jnp.float32)
+    link = link_ref[...]
+    sign = sign_ref[...]
+    for q, ref in enumerate((psi_ref, heat_ref, mag_ref, speed_ref)):
+        for c in range(2):
+            plain = ref[c, 0]
+            sets = [(2 * q + c, plain)]
+            if q < 3:
+                sets.append((8 + 2 * q + c, plain * degree))
+                sets.append((16 + 2 * q + c, pltpu.roll(plain * link, degrees - 1, 1)))
+            for row, value in sets:
+                signed = value * sign
+                for a in range(degrees // 128):
+                    cut = slice(a * 128, (a + 1) * 128)
+                    coef[a, pl.ds(row, group, stride=SET_ROWS), :] = value[:, cut]
+                    coef[a, pl.ds(SET_ROWS // 2 + row, group, stride=SET_ROWS), :] = signed[:, cut]
+
+    cosine = jnp.broadcast_to(cos_ref[...], (group, north))
+    zero = jnp.zeros((group, north), jnp.float32)
+
+    def sweep(position, state):
+        before, current, log_scale = state
+        base = pl.multiple_of(position * 128, 128)
+        rise = rise_ref[:, pl.ds(base, 128)]
+        fall = fall_ref[:, pl.ds(base, 128)]
+        diag = diag_ref[:, pl.ds(base, 128)]
+        for part in range(4):
+            scale = jnp.exp(log_scale)
+            for offset in range(32):
+                i = part * 32 + offset
+                fresh = (
+                    rise[:, i : i + 1] * cosine * current
+                    - fall[:, i : i + 1] * before
+                    + diag[:, i : i + 1]
+                )
+                before, current = current, fresh
+                row = fresh * scale
+                start = pl.multiple_of((base + i) * group, group)
+                for a in range(north // 128):
+                    table[a, pl.ds(start, group), :] = row[:, a * 128 : (a + 1) * 128]
+            magnitude = jnp.maximum(jnp.abs(before), jnp.abs(current))
+            magnitude = jnp.where(magnitude > 0.0, magnitude, 1.0)
+            before = before / magnitude
+            current = current / magnitude
+            log_scale = log_scale + jnp.log(magnitude)
+        return before, current, log_scale
+
+    lax.fori_loop(0, degrees // 128, sweep, (zero, zero, log_ref[...]))
+
+    def one_order(m, carry):
+        values = jnp.concatenate(
+            [table[a, pl.ds(m, degrees, stride=group), :] for a in range(north // 128)], axis=1
+        )
+        high, low = halves(values)
+        high_ref[m] = high
+        low_ref[m] = low
+        start = pl.multiple_of(m * SET_ROWS, SET_ROWS)
+        rows = jnp.concatenate(
+            [coef[a, pl.ds(start, SET_ROWS), :] for a in range(degrees // 128)], axis=1
+        )
+        rows_high, rows_low = halves(rows)
+        both = dot(jnp.concatenate([rows_high, rows_low], axis=0), high)
+        result = both[:SET_ROWS] + both[SET_ROWS:] + dot(rows_high, low)
+        wide = jnp.broadcast_to(cos_ref[...], (8, north))
+        pieces = jnp.concatenate(
+            [
+                result[0:8],
+                wide * result[8:16] - result[16:24],
+                result[24:32],
+                -wide * result[32:40] - result[40:48],
+            ],
+            axis=0,
+        )
+        first = pl.multiple_of((step * group + m) * PROFILE_ROWS, PROFILE_ROWS)
+        for a in range(north // 128):
+            prof[a, pl.ds(first, PROFILE_ROWS), :] = pieces[:, a * 128 : (a + 1) * 128]
+        return carry
+
+    lax.fori_loop(0, group, one_order, 0)
+
+    @pl.when(step == step_count - 1)
+    def _():
+        places = [0, 2, 4, 8, 10, 12, 6]
+        for side in range(2):
+            for q, place in enumerate(places):
+                first = side * 16 + place
+                for a in range(north // 128):
+                    block = jnp.concatenate(
+                        [
+                            prof[a, pl.ds(first + c, local, stride=PROFILE_ROWS), :]
+                            for c in range(2)
+                        ],
+                        axis=0,
+                    )
+                    turned = block.T
+                    lat = a * 128
+                    while lat < (a + 1) * 128:
+                        target, offset = divmod(lat, half)
+                        count = min(half - offset, (a + 1) * 128 - lat)
+                        out_ref[target, q, pl.ds(side * half + offset, count), :] = turned[
+                            lat - a * 128 : lat - a * 128 + count
+                        ]
+                        lat += count
+
+
+def synthesis(spectra, link, sign, rise, fall, diag, log_start, cosine, step_count, targets):
+    local, degrees = link.shape
+    north = cosine.shape[1]
+    group = local // step_count
+    spec = pl.BlockSpec((2, 1, group, degrees), lambda g: (0, 0, g, 0))
+    table_spec = pl.BlockSpec((group, degrees), lambda g: (g, 0))
+    legendre_spec = pl.BlockSpec((group, degrees, north), lambda g: (g, 0, 0))
+    out_shape = (targets, 7, 2 * (north // targets), 2 * local)
+    return pl.pallas_call(
+        functools.partial(synthesis_kernel, step_count=step_count),
+        grid=(step_count,),
+        in_specs=[spec] * 4
+        + [table_spec] * 5
+        + [
+            pl.BlockSpec((group, north), lambda g: (g, 0)),
+            pl.BlockSpec((1, north), lambda g: (0, 0)),
+        ],
+        out_specs=[
+            pl.BlockSpec(out_shape, lambda g: (0, 0, 0, 0)),
+            legendre_spec,
+            legendre_spec,
+        ],
+        out_shape=[
+            jax.ShapeDtypeStruct(out_shape, jnp.float32),
+            jax.ShapeDtypeStruct((local, degrees, north), jnp.bfloat16),
+            jax.ShapeDtypeStruct((local, degrees, north), jnp.bfloat16),
+        ],
+        scratch_shapes=[
+            pltpu.VMEM((north // 128, group * degrees, 128), jnp.float32),
+            pltpu.VMEM((degrees // 128, group * SET_ROWS, 128), jnp.float32),
+            pltpu.VMEM((north // 128, local * PROFILE_ROWS, 128), jnp.float32),
+        ],
+        compiler_params=pltpu.CompilerParams(vmem_limit_bytes=VMEM_BYTES),
+        cost_estimate=pl.CostEstimate(
+            flops=2 * 3 * SET_ROWS * local * degrees * north,
+            bytes_accessed=4 * local * degrees * north,
+            transcendentals=0,
+        ),
+        name="synthesis",
+    )(*spectra, link, sign, rise, fall, diag, log_start, cosine)
+
+
+def grid_kernel(
+    here_ref, above_ref, below_ref, weight_ref, spin_ref, high_ref, low_ref, factor_ref,
+    out_ref, sets, total, *, step_count, slope_scale, lon_total,
+):
+    step = pl.program_id(0)
+    sources, _, rows, lanes = here_ref.shape
+    count = 9 * rows
+
+    @pl.when(step == 0)
+    def _():
+        total[...] = jnp.zeros_like(total)
+        for source in range(sources):
+            cut = slice(source * lanes, (source + 1) * lanes)
+            weight = weight_ref[:, cut]
+            spin = spin_ref[:, cut]
+            for q in range(9):
+                if q < 3:
+                    value = pltpu.roll(here_ref[source, q], lanes // 2, 1) * spin
+                elif q < 7:
+                    value = here_ref[source, q] * weight
+                else:
+                    value = (above_ref[source, q - 7] - below_ref[source, q - 7]) * (
+                        weight * slope_scale
+                    )
+                high, low = halves(value)
+                sets[q * rows : (q + 1) * rows, cut] = high
+                sets[count + q * rows : count + (q + 1) * rows, cut] = low
+
+    both = dot(sets[...], high_ref[...])
+    grids = both[:count] + both[count:] + dot(sets[:count], low_ref[...])
+    g = [grids[q * rows : (q + 1) * rows] for q in range(9)]
+    factor = factor_ref[...]
+    heat = -((g[3] * g[1] - g[0] * g[4]) * factor + g[6] * g[7])
+    induction = -((g[3] * g[2] - g[0] * g[5]) * factor + g[6] * g[8])
+    high, low = halves(jnp.concatenate([heat, induction], axis=0))
+    back = dot_t(jnp.concatenate([high, low], axis=0), high_ref[...])
+    total[...] += back[: 2 * rows] + back[2 * rows :] + dot_t(high, low_ref[...])
+
+    @pl.when(step == step_count - 1)
+    def _():
+        for source in range(sources):
+            cut = slice(source * lanes, (source + 1) * lanes)
+            for f in range(2):
+                out_ref[source, f] = total[f * rows : (f + 1) * rows, cut] * (1.0 / lon_total)
+
+
+def grid_step(here, above, below, weight, spin, wave_high, wave_low, factor, slope_scale):
+    sources, _, rows, lanes = here.shape
+    waves, lon_total = wave_high.shape
+    lon_block = math.gcd(256, lon_total)
+    step_count = lon_total // lon_block
+    whole = lambda shape: pl.BlockSpec(shape, lambda i: (0,) * len(shape))
+    wave_spec = pl.BlockSpec((waves, lon_block), lambda i: (0, i))
+    out_shape = (sources, 2, rows, lanes)
+    return pl.pallas_call(
+        functools.partial(
+            grid_kernel, step_count=step_count, slope_scale=slope_scale, lon_total=lon_total
+        ),
+        grid=(step_count,),
+        in_specs=[
+            whole(here.shape), whole(above.shape), whole(below.shape),
+            whole(weight.shape), whole(spin.shape), wave_spec, wave_spec, whole(factor.shape),
+        ],
+        out_specs=whole(out_shape),
+        out_shape=jax.ShapeDtypeStruct(out_shape, jnp.float32),
+        scratch_shapes=[
+            pltpu.VMEM((18 * rows, waves), jnp.bfloat16),
+            pltpu.VMEM((2 * rows, waves), jnp.float32),
+        ],
+        compiler_params=pltpu.CompilerParams(vmem_limit_bytes=VMEM_BYTES),
+        cost_estimate=pl.CostEstimate(
+            flops=2 * 3 * 11 * rows * waves * lon_total,
+            bytes_accessed=4 * waves * lon_total,
+            transcendentals=0,
+        ),
+        name="grid_step",
+    )(here, above, below, weight, spin, wave_high, wave_low, factor)
+
+
+def analysis_kernel(
+    back_ref, quad_ref, sign_ref, heat_ref, mag_ref, high_ref, low_ref, out_ref,
+    values, tend, *, step_count,
+):
+    step = pl.program_id(0)
+    blocks, _, rows, lanes = back_ref.shape
+    half = rows // 2
+    local = lanes // 2
+    group = local // step_count
+    north = quad_ref.shape[1]
+
+    @pl.when(step == 0)
+    def _():
+        for f in range(2):
+            sides = []
+            for side in range(2):
+                stacked = jnp.concatenate(
+                    [back_ref[b, f, side * half : (side + 1) * half] for b in range(blocks)], axis=0
+                )
+                sides.append(stacked.T)
+            quad = quad_ref[...]
+            for sign, mixed in enumerate((sides[0] + sides[1], sides[0] - sides[1])):
+                mixed = mixed * quad
+                for c in range(2):
+                    row = sign * 4 + f * 2 + c
+                    for a in range(north // 128):
+                        values[a, pl.ds(row, local, stride=8), :] = mixed[
+                            c * local : (c + 1) * local, a * 128 : (a + 1) * 128
+                        ]
+
+    def one_order(m, carry):
+        start = pl.multiple_of((step * group + m) * 8, 8)
+        rows_in = jnp.concatenate(
+            [values[a, pl.ds(start, 8), :] for a in range(north // 128)], axis=1
+        )
+        row_high = rows_in.astype(jnp.bfloat16).astype(jnp.float32)
+        row_low = rows_in - row_high
+        both = jnp.concatenate([row_high, row_low], axis=0).astype(jnp.bfloat16)
+        first = dot_t(both, high_ref[m])
+        second = dot_t(both, low_ref[m])
+        result = first[:8] + first[8:] + second[:8]
+        for a in range(result.shape[1] // 128):
+            tend[a, pl.ds(pl.multiple_of(m * 8, 8), 8), :] = result[:, a * 128 : (a + 1) * 128]
+        return carry
+
+    lax.fori_loop(0, group, one_order, 0)
+    even = sign_ref[...] > 0.0
+    for f, ref in enumerate((heat_ref, mag_ref)):
+        for c in range(2):
+            parts = [
+                jnp.concatenate(
+                    [
+                        tend[a, pl.ds(sign * 4 + f * 2 + c, group, stride=8), :]
+                        for a in range(even.shape[1] // 128)
+                    ],
+                    axis=1,
+                )
+                for sign in range(2)
+            ]
+            out_ref[0, f, c] = ref[c, 0] + time_step * jnp.where(even, parts[0], parts[1])
+
+
+def analysis(back, quad, sign, heat, mag, high, low, step_count):
+    local, degrees, north = high.shape
+    group = local // step_count
+    spec = pl.BlockSpec((2, 1, group, degrees), lambda g: (0, 0, g, 0))
+    legendre_spec = pl.BlockSpec((group, degrees, north), lambda g: (g, 0, 0))
+    return pl.pallas_call(
+        functools.partial(analysis_kernel, step_count=step_count),
+        grid=(step_count,),
+        in_specs=[
+            pl.BlockSpec(back.shape, lambda g: (0, 0, 0, 0)),
+            pl.BlockSpec(quad.shape, lambda g: (0, 0)),
+            pl.BlockSpec((group, degrees), lambda g: (g, 0)),
+            spec, spec, legendre_spec, legendre_spec,
+        ],
+        out_specs=pl.BlockSpec((1, 2, 2, group, degrees), lambda g: (g, 0, 0, 0, 0)),
+        out_shape=jax.ShapeDtypeStruct((step_count, 2, 2, group, degrees), jnp.float32),
+        scratch_shapes=[
+            pltpu.VMEM((north // 128, local * 8, 128), jnp.float32),
+            pltpu.VMEM((degrees // 128, group * 8, 128), jnp.float32),
+        ],
+        compiler_params=pltpu.CompilerParams(vmem_limit_bytes=VMEM_BYTES),
+        cost_estimate=pl.CostEstimate(
+            flops=2 * 3 * 8 * local * degrees * north,
+            bytes_accessed=4 * local * degrees * north,
+            transcendentals=0,
+        ),
+        name="analysis",
+    )(back, quad, sign, heat, mag, high, low)
+
+
+def wave_halves(orders, lon_total):
+    width = 128
+    def pair(columns):
+        phase_int = orders[:, None] * columns[None, :] % lon_total
+        angle_vals = 2.0 * math.pi / lon_total * phase_int.astype(jnp.float32)
+        return jnp.cos(angle_vals), jnp.sin(angle_vals)
+
+    fine_cos, fine_sin = pair(jnp.arange(width, dtype=jnp.int32))
+    far_cos, far_sin = pair(jnp.arange(lon_total // width, dtype=jnp.int32) * width)
+    cos_parts, sin_parts = [], []
+    for a in range(lon_total // width):
+        ca, sa = far_cos[:, a : a + 1], far_sin[:, a : a + 1]
+        cos_parts.append(ca * fine_cos - sa * fine_sin)
+        sin_parts.append(-(sa * fine_cos + ca * fine_sin))
+    return jnp.concatenate(cos_parts, axis=1), jnp.concatenate(sin_parts, axis=1)
+
+
+def kernel_body(
+    toroidal_stream_spectra,
+    thermal_spectra,
+    induction_potential,
+    outward_speed_spectra,
+    position_azimuth_map,
+    subdiagonal_complement,
+    superdiagonal_complement,
+    diagonal_entries,
+):
+    row_count = lax.axis_size("row")
+    ma_count = lax.axis_size("ma")
+    local = thermal_spectra.shape[2]
+    degrees = thermal_spectra.shape[3]
+    north = NLAT // 2
+    half = north // ma_count
+    spacing = shell_span / row_count
+
+    small = jnp.stack([subdiagonal_complement, superdiagonal_complement, diagonal_entries])
+    row_index = lax.axis_index("row")
+    factors = jnp.zeros((row_count,) + small.shape, jnp.float32)
+    factors = lax.dynamic_update_slice_in_dim(factors, small[None], row_index, 0)
+    for shift in range(1, row_count):
+        moved = lax.ppermute(
+            small, "row", [(i, (i + shift) % row_count) for i in range(row_count)]
+        )
+        factors = lax.dynamic_update_slice_in_dim(
+            factors, moved[None], (row_index + row_count - shift) % row_count, 0
+        )
+    factors = factors[:, :, :, 0]
+
+    slot_start = lax.axis_index("ma") * local
+    my_orders = lax.dynamic_slice_in_dim(position_azimuth_map, slot_start, local)
+    order_col = my_orders.astype(jnp.float32)[:, None]
+    degree = jnp.arange(degrees, dtype=jnp.float32)[None, :]
+    degree_ints = jnp.arange(degrees, dtype=jnp.int32)
+    even_mask = (my_orders[:, None] + degree_ints[None, :]) % 2 == 0
+    sign = jnp.where(even_mask, 1.0, -1.0)
+    above_diag = degree > order_col
+    square = degree * degree - order_col * order_col
+    link = jnp.where(
+        above_diag,
+        jnp.sqrt(
+            jnp.maximum((2.0 * degree + 1.0) * square, 0.0) / jnp.maximum(2.0 * degree - 1.0, 1.0)
+        ),
+        0.0,
+    )
+    denominator = jnp.where(above_diag, square, 1.0)
+    rise = jnp.where(
+        above_diag, jnp.sqrt(jnp.maximum(4.0 * degree * degree - 1.0, 1.0) / denominator), 0.0
+    )
+    lower_term = (degree - 1.0) * (degree - 1.0) - order_col * order_col
+    fall = jnp.where(
+        above_diag,
+        jnp.sqrt(
+            jnp.maximum((2.0 * degree + 1.0) * lower_term, 0.0)
+            / (jnp.maximum(2.0 * degree - 3.0, 1.0) * denominator)
+        ),
+        0.0,
+    )
+    diag = jnp.where(degree == order_col, 1.0, 0.0)
+    theta = math.pi * (jnp.arange(NLAT, dtype=jnp.float32) + 0.5) / NLAT
+    cosine = jnp.cos(theta)[None, :north]
+    sine = jnp.sin(theta)[None, :north]
+    log_start = (
+        0.5 * (lax.lgamma(order_col + 1.5) - lax.lgamma(order_col + 1.0) - log_gamma_half)
+        - 0.5 * math.log(2.0)
+        + order_col * jnp.log(sine)
+    )
+    outgoing, high, low = synthesis(
+        (toroidal_stream_spectra, thermal_spectra, induction_potential, outward_speed_spectra),
+        link, sign, rise, fall, diag, log_start, cosine, row_count, ma_count,
+    )
+    here = lax.all_to_all(outgoing, "ma", 0, 0, tiled=True)
+
+    cos_wave, sin_wave = wave_halves(position_azimuth_map, NLON)
+    wave = jnp.stack(
+        [cos_wave.reshape(ma_count, local, NLON), sin_wave.reshape(ma_count, local, NLON)], axis=1
+    ).reshape(2 * ma_count * local, NLON)
+    rounded = lax.reduce_precision(wave, 8, 7)
+    wave_high = rounded.astype(jnp.bfloat16)
+    wave_low = (wave - rounded).astype(jnp.bfloat16)
+    orders = position_azimuth_map.astype(jnp.float32).reshape(ma_count, 1, local)
+    weight = jnp.where(orders == 0.0, 1.0, 2.0)
+    spin = jnp.concatenate([-orders * weight, orders * weight], axis=1).reshape(1, -1)
+    weight = jnp.concatenate([weight, weight], axis=1).reshape(1, -1)
+
+    forward = [(i, i + 1) for i in range(row_count - 1)]
+    backward = [(target, source) for source, target in forward]
+    profiles = here[:, 1:3]
+    below = lax.ppermute(profiles, "row", forward)
+    above = lax.ppermute(profiles, "row", backward)
+
+    lat_index = lax.axis_index("ma") * half + jnp.arange(half, dtype=jnp.int32)
+    sine_mine = jnp.sin(math.pi * (lat_index.astype(jnp.float32) + 0.5) / NLAT)
+    radius = inner_radius + spacing * (row_index.astype(jnp.float32) + 0.5)
+    factor = 1.0 / (radius * radius * (sine_mine * sine_mine))
+    factor = jnp.concatenate([factor, factor])[:, None]
+    spectra = grid_step(
+        here, above, below, weight, spin, wave_high, wave_low, factor, 1.0 / (2.0 * spacing)
+    )
+    back = lax.all_to_all(spectra, "ma", 0, 0, tiled=True)
+
+    quad = fejer_weights(north, NLAT)[None, :]
+    right_side = analysis(
+        back, quad, sign, thermal_spectra, induction_potential, high, low, row_count
+    )
+    shells = lax.all_to_all(right_side, "row", 0, 0, tiled=True)
+    spread = lambda k, which: factors[k, which][:, None, None, :]
+    running = jnp.zeros_like(shells[0])
+    scaled = []
+    for k in range(row_count):
+        running = shells[k] + (1.0 - spread(k, 0)) * running
+        scaled.append(running / spread(k, 2))
+    running = jnp.zeros_like(shells[0])
+    solved = []
+    for k in reversed(range(row_count)):
+        running = scaled[k] + (1.0 - spread(k, 1)) * running
+        solved.append(running)
+    solved = lax.all_to_all(jnp.stack(solved[::-1]), "row", 0, 0, tiled=True)
+    solved = jnp.transpose(solved, (1, 2, 0, 3, 4)).reshape(2, 2, 1, local, degrees)
+    return solved[0], solved[1]
+
+
+def program(*args):
+    row_count = lax.axis_size("row")
+    ma_count = lax.axis_size("ma")
+    _, shells, local, degrees = args[1].shape
+    fits = (
+        shells == 1
+        and (NLAT // 2) % (8 * ma_count) == 0
+        and (2 * local) % 128 == 0
+        and local % (16 * row_count) == 0
+        and degrees % 128 == 0
+        and (NLAT // 2) % 128 == 0
+        and NLON % 128 == 0
+    )
+    return kernel_body(*args) if fits else body(*args)
+
+
 def solution(mesh):
     in_specs = (
         P(None, "row", "ma", None),
@@ -321,4 +834,4 @@
         P(None, "row", None),
     )
     out_specs = (P(None, "row", "ma", None), P(None, "row", "ma", None))
-    return jax.shard_map(body, mesh=mesh, in_specs=in_specs, out_specs=out_specs, check_vma=False)
+    return jax.shard_map(program, mesh=mesh, in_specs=in_specs, out_specs=out_specs, check_vma=False)

time: 1040 us -> 240 us (0.23); the launches traced: 1020 us -> 240 us
  other arithmetic: 560 us -> 31.5 us
  local copies, waits for them, and re-layouts: 139 us -> 8.77 us
  Pallas kernels: 0 us -> 116 us
  matrix products: 114 us -> 0 us
  waiting for transfers between devices: 134 us -> 42.3 us
  loops' own time: 14.3 us -> 0 us
  between operations: 15.1 us -> 0.93 us
  blocking collectives: 28.6 us -> 17.3 us
    while x496 -> x0, other arithmetic: 360 us -> none
    pallas_call x0 -> x3, Pallas kernels: none -> 116 us  [the longest x1 68.7 us: synthesis(): pl.pallas_call(functools.partial(synthesis_kernel, step_count=step_count)...]
    dot_general x8 -> x0, matrix products: 114 us -> none  [the longest x1 45.5 us: body(): jnp.einsum('ocn,oln->ocl', stacked, legendre_all, precision=highest)]
    select_n x226 -> x2, other arithmetic: 101 us -> 1.8 us  [the longest x1 1.02 us: kernel_body(): jnp.where(above_diag, jnp.sqrt(jnp.maximum((2.0 * degree + 1.0) * lower_t...]
    all_gather x2 -> x0, waiting for transfers between devices: 67.3 us -> none  [entering_2(): gathered = jax.tree.map(lambda a: lax.all_gather(a, axis), part)]
    dynamic_update_slice x16 -> x4, local copies, waits for them, and re-layouts: 56.3 us -> 0.07 us  [the longest x3 0.05 us: kernel_body(): lax.dynamic_update_slice_in_dim(factors, moved[None], (row_index + row_co...]
    all_gather x2 -> x0, blocking collectives: 28.6 us -> none  [entering_2(): gathered = jax.tree.map(lambda a: lax.all_gather(a, axis), part)]
    cos x7 -> x2, other arithmetic: 25.9 us -> 0.27 us  [the longest x1 0.22 us: pair(): return (jnp.cos(angle_vals), jnp.sin(angle_vals))]
  transfers between devices with their start and end apart: 6 -> 8, of which waited for: 6 -> 5; matrix products, arithmetic and copies ran while one was open for 0% -> 15% of each run, Pallas kernels for 0% -> 48%
where the time goes in v1:
time: 240 us
  Pallas kernels  116 us (48%)
  waiting for transfers between devices  42.3 us (18%)
  other arithmetic  31.5 us (13%)
  starting transfers between devices  23.1 us (10%)
  blocking collectives  17.3 us (7%)
  local copies, waits for them, and re-layouts  8.77 us (4%)
    pallas_call x1, Pallas kernels, synthesis(): pl.pallas_call(functools.partial(synthesis_kernel, step_count=step_count)...  68.7 us
    pallas_call x1, Pallas kernels, analysis(): pl.pallas_call(functools.partial(analysis_kernel, step_count=step_count),...  26.6 us
    pallas_call x1, Pallas kernels, grid_step(): pl.pallas_call(functools.partial(grid_kernel, step_count=step_count, slop...  20.6 us
    all_to_all x1, blocking collectives, kernel_body(): solved = lax.all_to_all(jnp.stack(solved[::-1]), 'row', 0, 0, tiled=True)  17.3 us
    all_to_all x1, waiting for transfers between devices, kernel_body(): shells = lax.all_to_all(right_side, 'row', 0, 0, tiled=True)  14.6 us
    unnamed x11, other arithmetic  13.4 us
    all_to_all x1, waiting for transfers between devices, kernel_body(): here = lax.all_to_all(outgoing, 'ma', 0, 0, tiled=True)  9.8 us
    ppermute x1, waiting for transfers between devices, kernel_body(): above = lax.ppermute(profiles, 'row', backward)  9.14 us
  transfers between devices with their start and end apart: 8, of which 5 were waited for; matrix products, arithmetic and copies ran while one was open for 15% of the time, Pallas kernels for 48%

profile of v1, /device:TPU:2, one launch (start us, length us, event | category | flops | bytes accessed | tf_op | source)
XLA Modules:
  0.0 239.8 jit_solution(9830172049276406085)
XLA Ops:
  1.4 1.6 collective-permute-start.2
  3.0 2.6 %collective-permute-start.3 = (f32[3,2,1,512]{3,2,1,0:T(1,128)S(1)}, f32[3,2,1,512]{3,2,1,0:T(1,128)S(1)}, u32[]{:S(2)}, u32[]{:S(2)}) collective-permute-start(f32[3,2,1,512]{3,2,1,0:T(1,128)S(1)} %pad_maximum_fusion.2), channel_id=1, source_target_pairs={{0,16},{8,24},{16,0},{24,8},{1,17},{9,25},{17,1},{25,9},{2,18},{10... | collective-permute-start | bytes 36872 | tf_op jit(solution)/shard_map/ppermute | solution.py:708
  5.6 1.3 collective-permute-start.4
  11.0 68.7 %synthesis.1 = (f32[8,7,96,128]{3,2,1,0:T(8,128)}, bf16[64,512,384]{2,1,0:T(8,128)(2,1)}, bf16[64,512,384]{2,1,0:T(8,128)(2,1)}) custom-call(f32[2,1,64,512]{3,2,1,0:T(8,128)} %psi_ref.1, f32[2,1,64,512]{3,2,1,0:T(8,128)} %heat_ref.3, f32[2,1,64,512]{3,2,1,0:T(8,128)} %mag_ref.3, f32[2,1,64,512]{3,2,1,0:T(8,128)} %speed_ref.1, ...), custom_call_target="tpu_custom_call" | custom-call | flops 3623878656 | bytes 50331648 | tf_op jit(solution)/shard_map/synthesis/pallas_call | solution.py:463
  79.7 4.3 %all-to-all-start = ((f32[8,7,96,128]{3,2,1,0:T(8,128)}), f32[8,7,96,128]{3,2,1,0:T(8,128)S(1)}, u32[]{:S(2)}, u32[]{:S(2)}) async-start(f32[8,7,96,128]{3,2,1,0:T(8,128)} %get-tuple-element.5), calls=%async_computation | async-start | bytes 5505024 | tf_op jit(solution)/shard_map/all_to_all | solution.py:758
  89.8 1.2 subtract_dynamic-update-slice_fusion.10
  92.2 1.2 subtract_dynamic-update-slice_fusion.8
  94.6 1.2 subtract_dynamic-update-slice_fusion.6
  97.0 1.2 subtract_dynamic-update-slice_fusion.4
  99.4 1.4 subtract_dynamic-update-slice_fusion.2
  103.3 3.0 %pad_maximum_fusion = f32[8,2,64,1536]{3,2,1,0:T(8,128)} fusion(f32[8,1,64,1536]{3,2,1,0:T(8,128)S(1)} %get-tuple-element.59, f32[8,1,64,1536]{3,2,1,0:T(8,128)S(1)} %get-tuple-element.58), kind=kLoop, calls=%fused_computation.3 | loop fusion | flops 1572864 | bytes 12582912 | tf_op jit(solution)/shard_map/stack | solution.py:761
  106.3 9.8 %all-to-all-done.here_ref = f32[8,7,96,128]{3,2,1,0:T(8,128)S(1)} async-done(((f32[8,7,96,128]{3,2,1,0:T(8,128)}), f32[8,7,96,128]{3,2,1,0:T(8,128)S(1)}, u32[]{:S(2)}, u32[]{:S(2)}) %all-to-all-start) | async-done | bytes 2752544 | tf_op jit(solution)/shard_map/all_to_all | solution.py:758
  116.2 1.3 collective-permute-start
  117.5 4.6 %collective-permute-start.1 = (f32[8,2,96,128]{3,2,1,0:T(8,128)S(1)}, f32[8,2,96,128]{3,2,1,0:T(8,128)S(1)}, u32[]{:S(2)}, u32[]{:S(2)}) collective-permute-start(f32[8,2,96,128]{3,2,1,0:T(8,128)S(1)} %slice.182), channel_id=1, source_target_pairs={{0,8},{8,16},{16,24},{1,9},{9,17},{17,25},{2,10},{10,18},{18,26},{... | collective-permute-start | bytes 2359304 | tf_op jit(solution)/shard_map/ppermute | solution.py:775
  122.1 6.4 %fusion = (bf16[1024,1536]{1,0:T(8,128)(2,1)}, bf16[1024,1536]{1,0:T(8,128)(2,1)}) fusion(f32[8,2,64,1536]{3,2,1,0:T(8,128)} %pad_maximum_fusion), kind=kLoop, calls=%fused_computation.2 | loop fusion | flops 6291456 | bytes 12582912 | tf_op jit(solution)/shard_map/convert_element_type | solution.py:766
  128.4 9.1 %collective-permute-done.above_ref = f32[8,2,96,128]{3,2,1,0:T(8,128)S(1)} collective-permute-done((f32[8,2,96,128]{3,2,1,0:T(8,128)S(1)}, f32[8,2,96,128]{3,2,1,0:T(8,128)S(1)}, u32[]{:S(2)}, u32[]{:S(2)}) %collective-permute-start) | collective-permute-done | bytes 786464 | tf_op jit(solution)/shard_map/ppermute | solution.py:776
  139.7 20.6 %grid_step.1 = f32[8,2,96,128]{3,2,1,0:T(8,128)} custom-call(f32[8,7,96,128]{3,2,1,0:T(8,128)} %copy-done, f32[8,2,96,128]{3,2,1,0:T(8,128)} %copy-done.6, f32[8,2,96,128]{3,2,1,0:T(8,128)} %copy-done.7, f32[1,1024]{1,0:T(1,128)} %reshape.1236.weight_ref, f32[1,1024]{1,0:T(1,128)} %reshape.1237.spin_ref, bf16[1024,1536]{1,0:T(8,128)(2,1)} %get-tuple-element.43.high_ref, ...), custom_call_target="tpu_custom_call" | custom-call | flops 9965666304 | bytes 6291456 | tf_op jit(solution)/shard_map/grid_step/pallas_call | solution.py:551
  160.3 3.5 %all-to-all-start.1 = ((f32[8,2,96,128]{3,2,1,0:T(8,128)}), f32[8,2,96,128]{3,2,1,0:T(8,128)S(1)}, u32[]{:S(2)}, u32[]{:S(2)}) async-start(f32[8,2,96,128]{3,2,1,0:T(8,128)} %grid_step.1), calls=%async_computation.1 | async-start | bytes 1572864 | tf_op jit(solution)/shard_map/all_to_all | solution.py:786
  163.8 2.7 %fusion.7 = f32[384]{0:T(512)S(1)} fusion(f32[384]{0:T(512)S(1)} %fusion.57, s32[384]{0:T(512)S(1)} %get-tuple-element.99, s32[384]{0:T(512)S(1)} %get-tuple-element.100), kind=kLoop, calls=%fused_computation.12 | loop fusion | flops 1621632 | bytes 6144 | tf_op jit(solution)/shard_map/reduce_sum | solution.py:161
  167.1 7.6 %all-to-all-done.1.back_ref = f32[8,2,96,128]{3,2,1,0:T(8,128)S(1)} async-done(((f32[8,2,96,128]{3,2,1,0:T(8,128)}), f32[8,2,96,128]{3,2,1,0:T(8,128)S(1)}, u32[]{:S(2)}, u32[]{:S(2)}) %all-to-all-start.1) | async-done | bytes 786464 | tf_op jit(solution)/shard_map/all_to_all | solution.py:786
  175.6 26.6 %analysis.1 = f32[4,2,2,16,512]{4,3,2,1,0:T(8,128)} custom-call(f32[8,2,96,128]{3,2,1,0:T(8,128)} %copy-done.1, f32[1,384]{1,0:T(1,128)} %mul.1425.quad_ref, f32[64,512]{1,0:T(8,128)} %fusion.33.sign_ref, f32[2,1,64,512]{3,2,1,0:T(8,128)} %heat_ref.3, f32[2,1,64,512]{3,2,1,0:T(8,128)} %mag_ref.3, bf16[64,512,384]{2,1,0:T(8,128)(2,1)} %get-tuple-element.6.high_ref, ...), custom_call_target="tpu_custom_call" | custom-call | flops 603979776 | bytes 50331648 | tf_op jit(solution)/shard_map/analysis/pallas_call | solution.py:643
  202.2 3.8 %all-to-all-start.2 = ((f32[4,2,2,16,512]{4,3,2,1,0:T(8,128)}), f32[4,2,2,16,512]{4,3,2,1,0:T(8,128)S(1)}, u32[]{:S(2)}, u32[]{:S(2)}) async-start(f32[4,2,2,16,512]{4,3,2,1,0:T(8,128)} %analysis.1), calls=%async_computation.2 | async-start | bytes 1048576 | tf_op jit(solution)/shard_map/all_to_all | solution.py:792
  206.2 14.6 %all-to-all-done.2 = f32[4,2,2,16,512]{4,3,2,1,0:T(8,128)S(1)} async-done(((f32[4,2,2,16,512]{4,3,2,1,0:T(8,128)}), f32[4,2,2,16,512]{4,3,2,1,0:T(8,128)S(1)}, u32[]{:S(2)}, u32[]{:S(2)}) %all-to-all-start.2) | async-done | bytes 524320 | tf_op jit(solution)/shard_map/all_to_all | solution.py:792
  221.0 17.3 %all_to_all.20 = f32[4,2,2,16,512]{4,3,2,1,0:T(8,128)S(1)} all-to-all(f32[4,2,2,16,512]{4,3,2,1,0:T(8,128)S(1)} %pad_maximum_fusion.1), channel_id=1, replica_groups=mesh['row'=4,'ma'=8] {'row'}, dimensions={0} | all-to-all | bytes 1048576 | tf_op jit(solution)/shard_map/all_to_all | solution.py:804
  (97 shorter events, 23.1 us)
Async XLA Ops:
  1.4 204.7 %collective-permute-start.2 = (f32[3,2,1,512]{3,2,1,0:T(1,128)S(1)}, f32[3,2,1,512]{3,2,1,0:T(1,128)S(1)}, u32[]{:S(2)}, u32[]{:S(2)}) collective-permute-start(f32[3,2,1,512]{3,2,1,0:T(1,128)S(1)} %pad_maximum_fusion.2), channel_id=1, source_target_pairs={{0,8},{8,16},{16,24},{24,0},{1,9},{9,17},{17,25},{25,1},{2,10},{10... | collective-permute-start | bytes 36872 | tf_op jit(solution)/shard_map/ppermute | solution.py:708
  3.0 203.1 %collective-permute-start.3 = (f32[3,2,1,512]{3,2,1,0:T(1,128)S(1)}, f32[3,2,1,512]{3,2,1,0:T(1,128)S(1)}, u32[]{:S(2)}, u32[]{:S(2)}) collective-permute-start(f32[3,2,1,512]{3,2,1,0:T(1,128)S(1)} %pad_maximum_fusion.2), channel_id=1, source_target_pairs={{0,16},{8,24},{16,0},{24,8},{1,17},{9,25},{17,1},{25,9},{2,18},{10... | collective-permute-start | bytes 36872 | tf_op jit(solution)/shard_map/ppermute | solution.py:708
  5.6 200.5 %collective-permute-start.4 = (f32[3,2,1,512]{3,2,1,0:T(1,128)S(1)}, f32[3,2,1,512]{3,2,1,0:T(1,128)S(1)}, u32[]{:S(2)}, u32[]{:S(2)}) collective-permute-start(f32[3,2,1,512]{3,2,1,0:T(1,128)S(1)} %pad_maximum_fusion.2), channel_id=1, source_target_pairs={{0,24},{8,0},{16,8},{24,16},{1,25},{9,1},{17,9},{25,17},{2,26},{10... | collective-permute-start | bytes 36872 | tf_op jit(solution)/shard_map/ppermute | solution.py:708
  79.7 4.3 %copy-start.2 = (s32[512]{0:T(512)S(1)}, s32[512]{0:T(512)}, u32[]{:S(2)}) copy-start(s32[512]{0:T(512)} %param.12) | copy-start | bytes 6148
  79.7 36.4 %all-to-all-start = ((f32[8,7,96,128]{3,2,1,0:T(8,128)}), f32[8,7,96,128]{3,2,1,0:T(8,128)S(1)}, u32[]{:S(2)}, u32[]{:S(2)}) async-start(f32[8,7,96,128]{3,2,1,0:T(8,128)} %get-tuple-element.5), calls=%async_computation | async-start | bytes 5505024 | tf_op jit(solution)/shard_map/all_to_all | solution.py:758
  116.1 12.3 %copy-start = (f32[8,7,96,128]{3,2,1,0:T(8,128)}, f32[8,7,96,128]{3,2,1,0:T(8,128)S(1)}, u32[]{:S(2)}) copy-start(f32[8,7,96,128]{3,2,1,0:T(8,128)S(1)} %all-to-all-done.here_ref) | copy-start | bytes 8257540
  116.2 21.4 %collective-permute-start = (f32[8,2,96,128]{3,2,1,0:T(8,128)S(1)}, f32[8,2,96,128]{3,2,1,0:T(8,128)S(1)}, u32[]{:S(2)}, u32[]{:S(2)}) collective-permute-start(f32[8,2,96,128]{3,2,1,0:T(8,128)S(1)} %slice.182), channel_id=1, source_target_pairs={{8,0},{16,8},{24,16},{9,1},{17,9},{25,17},{10,2},{18,10},{26,18},{... | collective-permute-start | bytes 2359304 | tf_op jit(solution)/shard_map/ppermute | solution.py:776
  117.5 21.3 %collective-permute-start.1 = (f32[8,2,96,128]{3,2,1,0:T(8,128)S(1)}, f32[8,2,96,128]{3,2,1,0:T(8,128)S(1)}, u32[]{:S(2)}, u32[]{:S(2)}) collective-permute-start(f32[8,2,96,128]{3,2,1,0:T(8,128)S(1)} %slice.182), channel_id=1, source_target_pairs={{0,8},{8,16},{16,24},{1,9},{9,17},{17,25},{2,10},{10,18},{18,26},{... | collective-permute-start | bytes 2359304 | tf_op jit(solution)/shard_map/ppermute | solution.py:775
  137.6 1.2 copy-start.6
  138.8 0.9 copy-start.7
  139.7 27.4 %copy-start.3 = (f32[2,1,512]{2,1,0:T(1,128)S(1)}, f32[2,1,512]{2,1,0:T(1,128)}, u32[]{:S(2)}) copy-start(f32[2,1,512]{2,1,0:T(1,128)} %param.15) | copy-start | bytes 12292
  139.7 27.4 %copy-start.4 = (f32[2,1,512]{2,1,0:T(1,128)S(1)}, f32[2,1,512]{2,1,0:T(1,128)}, u32[]{:S(2)}) copy-start(f32[2,1,512]{2,1,0:T(1,128)} %param.14) | copy-start | bytes 12292
  139.7 27.4 %copy-start.5 = (f32[2,1,512]{2,1,0:T(1,128)S(1)}, f32[2,1,512]{2,1,0:T(1,128)}, u32[]{:S(2)}) copy-start(f32[2,1,512]{2,1,0:T(1,128)} %param.13) | copy-start | bytes 12292
  160.3 14.4 %all-to-all-start.1 = ((f32[8,2,96,128]{3,2,1,0:T(8,128)}), f32[8,2,96,128]{3,2,1,0:T(8,128)S(1)}, u32[]{:S(2)}, u32[]{:S(2)}) async-start(f32[8,2,96,128]{3,2,1,0:T(8,128)} %grid_step.1), calls=%async_computation.1 | async-start | bytes 1572864 | tf_op jit(solution)/shard_map/all_to_all | solution.py:786
  174.7 0.9 copy-start.1
  202.2 18.6 %all-to-all-start.2 = ((f32[4,2,2,16,512]{4,3,2,1,0:T(8,128)}), f32[4,2,2,16,512]{4,3,2,1,0:T(8,128)S(1)}, u32[]{:S(2)}, u32[]{:S(2)}) async-start(f32[4,2,2,16,512]{4,3,2,1,0:T(8,128)} %analysis.1), calls=%async_computation.2 | async-start | bytes 1048576 | tf_op jit(solution)/shard_map/all_to_all | solution.py:792

commit v2 on v1

--- a/solution.py
+++ b/solution.py
@@ -334,14 +334,18 @@
 
 def synthesis_kernel(
     psi_ref, heat_ref, mag_ref, speed_ref, link_ref, sign_ref, rise_ref, fall_ref, diag_ref,
-    log_ref, cos_ref, out_ref, high_ref, low_ref, table, coef, prof, *, step_count,
+    log_ref, cos_ref, pair_ref, rest_ref, high_ref, low_ref, even_table, odd_table, coef, prof,
+    *, step_count,
 ):
     step = pl.program_id(0)
     group, degrees = link_ref.shape
     north = cos_ref.shape[1]
     local = group * step_count
-    targets, quantities, rows, lanes = out_ref.shape
-    half = rows // 2
+    half = pair_ref.shape[2] // 2
+    done_group = jnp.maximum(step - 1, 0)
+    tiles = north // 128
+    sweeps = degrees // 128
+    orders_each = group // sweeps
 
     @pl.when(step == 0)
     def _():
@@ -359,81 +363,88 @@
                 sets.append((16 + 2 * q + c, pltpu.roll(plain * link, degrees - 1, 1)))
             for row, value in sets:
                 signed = value * sign
-                for a in range(degrees // 128):
+                for a in range(sweeps):
                     cut = slice(a * 128, (a + 1) * 128)
                     coef[a, pl.ds(row, group, stride=SET_ROWS), :] = value[:, cut]
                     coef[a, pl.ds(SET_ROWS // 2 + row, group, stride=SET_ROWS), :] = signed[:, cut]
 
-    cosine = jnp.broadcast_to(cos_ref[...], (group, north))
-    zero = jnp.zeros((group, north), jnp.float32)
-
-    def sweep(position, state):
-        before, current, log_scale = state
-        base = pl.multiple_of(position * 128, 128)
-        rise = rise_ref[:, pl.ds(base, 128)]
-        fall = fall_ref[:, pl.ds(base, 128)]
-        diag = diag_ref[:, pl.ds(base, 128)]
-        for part in range(4):
-            scale = jnp.exp(log_scale)
-            for offset in range(32):
-                i = part * 32 + offset
-                fresh = (
-                    rise[:, i : i + 1] * cosine * current
-                    - fall[:, i : i + 1] * before
-                    + diag[:, i : i + 1]
-                )
-                before, current = current, fresh
-                row = fresh * scale
-                start = pl.multiple_of((base + i) * group, group)
-                for a in range(north // 128):
-                    table[a, pl.ds(start, group), :] = row[:, a * 128 : (a + 1) * 128]
-            magnitude = jnp.maximum(jnp.abs(before), jnp.abs(current))
-            magnitude = jnp.where(magnitude > 0.0, magnitude, 1.0)
-            before = before / magnitude
-            current = current / magnitude
-            log_scale = log_scale + jnp.log(magnitude)
-        return before, current, log_scale
-
-    lax.fori_loop(0, degrees // 128, sweep, (zero, zero, log_ref[...]))
-
-    def one_order(m, carry):
-        values = jnp.concatenate(
-            [table[a, pl.ds(m, degrees, stride=group), :] for a in range(north // 128)], axis=1
-        )
-        high, low = halves(values)
-        high_ref[m] = high
-        low_ref[m] = low
-        start = pl.multiple_of(m * SET_ROWS, SET_ROWS)
-        rows = jnp.concatenate(
-            [coef[a, pl.ds(start, SET_ROWS), :] for a in range(degrees // 128)], axis=1
-        )
-        rows_high, rows_low = halves(rows)
-        both = dot(jnp.concatenate([rows_high, rows_low], axis=0), high)
-        result = both[:SET_ROWS] + both[SET_ROWS:] + dot(rows_high, low)
+    def run(fill, ready):
+        cosine = jnp.broadcast_to(cos_ref[...], (group, north))
         wide = jnp.broadcast_to(cos_ref[...], (8, north))
-        pieces = jnp.concatenate(
-            [
-                result[0:8],
-                wide * result[8:16] - result[16:24],
-                result[24:32],
-                -wide * result[32:40] - result[40:48],
-            ],
-            axis=0,
-        )
-        first = pl.multiple_of((step * group + m) * PROFILE_ROWS, PROFILE_ROWS)
-        for a in range(north // 128):
-            prof[a, pl.ds(first, PROFILE_ROWS), :] = pieces[:, a * 128 : (a + 1) * 128]
-        return carry
-
-    lax.fori_loop(0, group, one_order, 0)
-
-    @pl.when(step == step_count - 1)
+        zero = jnp.zeros((group, north), jnp.float32)
+
+        def one_order(m):
+            values = jnp.concatenate(
+                [ready[a, pl.ds(m, degrees, stride=group), :] for a in range(tiles)], axis=1
+            )
+            high, low = halves(values)
+            high_ref[m] = high
+            low_ref[m] = low
+            start = pl.multiple_of(m * SET_ROWS, SET_ROWS)
+            rows = jnp.concatenate(
+                [coef[a, pl.ds(start, SET_ROWS), :] for a in range(sweeps)], axis=1
+            )
+            rows_high, rows_low = halves(rows)
+            both = dot(jnp.concatenate([rows_high, rows_low], axis=0), high)
+            result = both[:SET_ROWS] + both[SET_ROWS:] + dot(rows_high, low)
+            pieces = jnp.concatenate(
+                [
+                    result[0:8],
+                    wide * result[8:16] - result[16:24],
+                    result[24:32],
+                    -wide * result[32:40] - result[40:48],
+                ],
+                axis=0,
+            )
+            first = pl.multiple_of((done_group * group + m) * PROFILE_ROWS, PROFILE_ROWS)
+            for a in range(tiles):
+                prof[a, pl.ds(first, PROFILE_ROWS), :] = pieces[:, a * 128 : (a + 1) * 128]
+
+        def sweep(position, state):
+            before, current, log_scale = state
+            base = pl.multiple_of(position * 128, 128)
+            rise = rise_ref[:, pl.ds(base, 128)]
+            fall = fall_ref[:, pl.ds(base, 128)]
+            diag = diag_ref[:, pl.ds(base, 128)]
+            for part in range(4):
+                if part * orders_each % 4 == 0:
+                    one_order(position * orders_each + part * orders_each // 4)
+                scale = jnp.exp(log_scale)
+                for offset in range(32):
+                    i = part * 32 + offset
+                    fresh = rise[:, i : i + 1] * cosine * current + (
+                        diag[:, i : i + 1] - fall[:, i : i + 1] * before
+                    )
+                    before, current = current, fresh
+                    row = fresh * scale
+                    start = pl.multiple_of((base + i) * group, group)
+                    for a in range(tiles):
+                        fill[a, pl.ds(start, group), :] = row[:, a * 128 : (a + 1) * 128]
+                magnitude = jnp.maximum(jnp.abs(before), jnp.abs(current))
+                magnitude = jnp.where(magnitude > 0.0, magnitude, 1.0)
+                before = before / magnitude
+                current = current / magnitude
+                log_scale = log_scale + jnp.log(magnitude)
+            return before, current, log_scale
+
+        lax.fori_loop(0, sweeps, sweep, (zero, zero, log_ref[...]))
+
+    @pl.when(step % 2 == 0)
     def _():
-        places = [0, 2, 4, 8, 10, 12, 6]
+        run(even_table, odd_table)
+
+    @pl.when(step % 2 == 1)
+    def _():
+        run(odd_table, even_table)
+
+    @pl.when(step == step_count)
+    def _():
+        places = [2, 4, 0, 8, 10, 12, 6]
         for side in range(2):
             for q, place in enumerate(places):
+                target_ref, slot = (pair_ref, q) if q < 2 else (rest_ref, q - 2)
                 first = side * 16 + place
-                for a in range(north // 128):
+                for a in range(tiles):
                     block = jnp.concatenate(
                         [
                             prof[a, pl.ds(first + c, local, stride=PROFILE_ROWS), :]
@@ -446,41 +457,52 @@
                     while lat < (a + 1) * 128:
                         target, offset = divmod(lat, half)
                         count = min(half - offset, (a + 1) * 128 - lat)
-                        out_ref[target, q, pl.ds(side * half + offset, count), :] = turned[
+                        target_ref[target, slot, pl.ds(side * half + offset, count), :] = turned[
                             lat - a * 128 : lat - a * 128 + count
                         ]
                         lat += count
 
 
-def synthesis(spectra, link, sign, rise, fall, diag, log_start, cosine, step_count, targets):
+def synthesis(spectra, link, sign, rise, fall, diag, log_start, cosine, targets):
     local, degrees = link.shape
     north = cosine.shape[1]
-    group = local // step_count
-    spec = pl.BlockSpec((2, 1, group, degrees), lambda g: (0, 0, g, 0))
-    table_spec = pl.BlockSpec((group, degrees), lambda g: (g, 0))
-    legendre_spec = pl.BlockSpec((group, degrees, north), lambda g: (g, 0, 0))
-    out_shape = (targets, 7, 2 * (north // targets), 2 * local)
+    group = 8
+    step_count = local // group
+    done = lambda g: jnp.maximum(g - 1, 0)
+    fresh = lambda g: jnp.minimum(g, step_count - 1)
+    spec = pl.BlockSpec((2, 1, group, degrees), lambda g: (0, 0, done(g), 0))
+    done_spec = pl.BlockSpec((group, degrees), lambda g: (done(g), 0))
+    fresh_spec = pl.BlockSpec((group, degrees), lambda g: (fresh(g), 0))
+    legendre_spec = pl.BlockSpec((group, degrees, north), lambda g: (done(g), 0, 0))
+    rows = 2 * (north // targets)
+    pair_shape = (targets, 2, rows, 2 * local)
+    rest_shape = (targets, 5, rows, 2 * local)
+    table = pltpu.VMEM((north // 128, group * degrees, 128), jnp.float32)
     return pl.pallas_call(
         functools.partial(synthesis_kernel, step_count=step_count),
-        grid=(step_count,),
+        grid=(step_count + 1,),
         in_specs=[spec] * 4
-        + [table_spec] * 5
+        + [done_spec] * 2
+        + [fresh_spec] * 3
         + [
-            pl.BlockSpec((group, north), lambda g: (g, 0)),
+            pl.BlockSpec((group, north), lambda g: (fresh(g), 0)),
             pl.BlockSpec((1, north), lambda g: (0, 0)),
         ],
         out_specs=[
-            pl.BlockSpec(out_shape, lambda g: (0, 0, 0, 0)),
+            pl.BlockSpec(pair_shape, lambda g: (0, 0, 0, 0)),
+            pl.BlockSpec(rest_shape, lambda g: (0, 0, 0, 0)),
             legendre_spec,
             legendre_spec,
         ],
         out_shape=[
-            jax.ShapeDtypeStruct(out_shape, jnp.float32),
+            jax.ShapeDtypeStruct(pair_shape, jnp.float32),
+            jax.ShapeDtypeStruct(rest_shape, jnp.float32),
             jax.ShapeDtypeStruct((local, degrees, north), jnp.bfloat16),
             jax.ShapeDtypeStruct((local, degrees, north), jnp.bfloat16),
         ],
         scratch_shapes=[
-            pltpu.VMEM((north // 128, group * degrees, 128), jnp.float32),
+            table,
+            table,
             pltpu.VMEM((degrees // 128, group * SET_ROWS, 128), jnp.float32),
             pltpu.VMEM((north // 128, local * PROFILE_ROWS, 128), jnp.float32),
         ],
@@ -495,11 +517,11 @@
 
 
 def grid_kernel(
-    here_ref, above_ref, below_ref, weight_ref, spin_ref, high_ref, low_ref, factor_ref,
+    pair_ref, rest_ref, above_ref, below_ref, weight_ref, spin_ref, high_ref, low_ref, factor_ref,
     out_ref, sets, total, *, step_count, slope_scale, lon_total,
 ):
     step = pl.program_id(0)
-    sources, _, rows, lanes = here_ref.shape
+    sources, _, rows, lanes = pair_ref.shape
     count = 9 * rows
 
     @pl.when(step == 0)
@@ -511,9 +533,10 @@
             spin = spin_ref[:, cut]
             for q in range(9):
                 if q < 3:
-                    value = pltpu.roll(here_ref[source, q], lanes // 2, 1) * spin
+                    plain = pair_ref[source, q - 1] if q else rest_ref[source, 0]
+                    value = pltpu.roll(plain, lanes // 2, 1) * spin
                 elif q < 7:
-                    value = here_ref[source, q] * weight
+                    value = rest_ref[source, q - 2] * weight
                 else:
                     value = (above_ref[source, q - 7] - below_ref[source, q - 7]) * (
                         weight * slope_scale
@@ -540,8 +563,8 @@
                 out_ref[source, f] = total[f * rows : (f + 1) * rows, cut] * (1.0 / lon_total)
 
 
-def grid_step(here, above, below, weight, spin, wave_high, wave_low, factor, slope_scale):
-    sources, _, rows, lanes = here.shape
+def grid_step(pair, rest, above, below, weight, spin, wave_high, wave_low, factor, slope_scale):
+    sources, _, rows, lanes = pair.shape
     waves, lon_total = wave_high.shape
     lon_block = math.gcd(256, lon_total)
     step_count = lon_total // lon_block
@@ -554,7 +577,7 @@
         ),
         grid=(step_count,),
         in_specs=[
-            whole(here.shape), whole(above.shape), whole(below.shape),
+            whole(pair.shape), whole(rest.shape), whole(above.shape), whole(below.shape),
             whole(weight.shape), whole(spin.shape), wave_spec, wave_spec, whole(factor.shape),
         ],
         out_specs=whole(out_shape),
@@ -570,7 +593,7 @@
             transcendentals=0,
         ),
         name="grid_step",
-    )(here, above, below, weight, spin, wave_high, wave_low, factor)
+    )(pair, rest, above, below, weight, spin, wave_high, wave_low, factor)
 
 
 def analysis_kernel(
@@ -700,19 +723,7 @@
     half = north // ma_count
     spacing = shell_span / row_count
 
-    small = jnp.stack([subdiagonal_complement, superdiagonal_complement, diagonal_entries])
     row_index = lax.axis_index("row")
-    factors = jnp.zeros((row_count,) + small.shape, jnp.float32)
-    factors = lax.dynamic_update_slice_in_dim(factors, small[None], row_index, 0)
-    for shift in range(1, row_count):
-        moved = lax.ppermute(
-            small, "row", [(i, (i + shift) % row_count) for i in range(row_count)]
-        )
-        factors = lax.dynamic_update_slice_in_dim(
-            factors, moved[None], (row_index + row_count - shift) % row_count, 0
-        )
-    factors = factors[:, :, :, 0]
-
     slot_start = lax.axis_index("ma") * local
     my_orders = lax.dynamic_slice_in_dim(position_azimuth_map, slot_start, local)
     order_col = my_orders.astype(jnp.float32)[:, None]
@@ -751,11 +762,13 @@
         - 0.5 * math.log(2.0)
         + order_col * jnp.log(sine)
     )
-    outgoing, high, low = synthesis(
+    pair, rest, high, low = synthesis(
         (toroidal_stream_spectra, thermal_spectra, induction_potential, outward_speed_spectra),
-        link, sign, rise, fall, diag, log_start, cosine, row_count, ma_count,
-    )
-    here = lax.all_to_all(outgoing, "ma", 0, 0, tiled=True)
+        link, sign, rise, fall, diag, log_start, cosine, ma_count,
+    )
+    pair = lax.all_to_all(pair, "ma", 0, 0, tiled=True)
+    pair, rest = lax.optimization_barrier((pair, rest))
+    rest = lax.all_to_all(rest, "ma", 0, 0, tiled=True)
 
     cos_wave, sin_wave = wave_halves(position_azimuth_map, NLON)
     wave = jnp.stack(
@@ -771,9 +784,8 @@
 
     forward = [(i, i + 1) for i in range(row_count - 1)]
     backward = [(target, source) for source, target in forward]
-    profiles = here[:, 1:3]
-    below = lax.ppermute(profiles, "row", forward)
-    above = lax.ppermute(profiles, "row", backward)
+    below = lax.ppermute(pair, "row", forward)
+    above = lax.ppermute(pair, "row", backward)
 
     lat_index = lax.axis_index("ma") * half + jnp.arange(half, dtype=jnp.int32)
     sine_mine = jnp.sin(math.pi * (lat_index.astype(jnp.float32) + 0.5) / NLAT)
@@ -781,8 +793,21 @@
     factor = 1.0 / (radius * radius * (sine_mine * sine_mine))
     factor = jnp.concatenate([factor, factor])[:, None]
     spectra = grid_step(
-        here, above, below, weight, spin, wave_high, wave_low, factor, 1.0 / (2.0 * spacing)
-    )
+        pair, rest, above, below, weight, spin, wave_high, wave_low, factor, 1.0 / (2.0 * spacing)
+    )
+    small = jnp.stack([subdiagonal_complement, superdiagonal_complement, diagonal_entries])
+    small, spectra = lax.optimization_barrier((small, spectra))
+    factors = jnp.zeros((row_count,) + small.shape, jnp.float32)
+    factors = lax.dynamic_update_slice_in_dim(factors, small[None], row_index, 0)
+    for shift in range(1, row_count):
+        moved = lax.ppermute(
+            small, "row", [(i, (i + shift) % row_count) for i in range(row_count)]
+        )
+        factors = lax.dynamic_update_slice_in_dim(
+            factors, moved[None], (row_index + row_count - shift) % row_count, 0
+        )
+    factors = factors[:, :, :, 0]
+
     back = lax.all_to_all(spectra, "ma", 0, 0, tiled=True)
 
     quad = fejer_weights(north, NLAT)[None, :]
@@ -816,6 +841,7 @@
         and (2 * local) % 128 == 0
         and local % (16 * row_count) == 0
         and degrees % 128 == 0
+        and 8 % (degrees // 128) == 0
         and (NLAT // 2) % 128 == 0
         and NLON % 128 == 0
     )

time: 240 us -> 219 us (0.912)
  Pallas kernels: 116 us -> 94.6 us
  waiting for transfers between devices: 42.3 us -> 34.2 us
  other arithmetic: 31.5 us -> 36.7 us
  starting transfers between devices: 23.1 us -> 26.8 us
    pallas_call x1, Pallas kernels: 68.7 us -> 47.3 us  [synthesis(): pl.pallas_call(functools.partial(synthesis_kernel, step_count=step_count)...]
    all_to_all x1 -> x2, waiting for transfers between devices: 9.8 us -> 0.01 us  [the longest x1 0.01 us: kernel_body(): pair = lax.all_to_all(pair, 'ma', 0, 0, tiled=True)]
    unnamed x11, other arithmetic: 13.4 us -> 22 us
    ppermute x2, waiting for transfers between devices: 10.3 us -> 16.4 us  [the longest x1 12.3 us: kernel_body(): below = lax.ppermute(pair, 'row', forward)]
    all_to_all x1 -> x2, starting transfers between devices: 4.27 us -> 8.65 us  [the longest x1 4.35 us: kernel_body(): pair = lax.all_to_all(pair, 'ma', 0, 0, tiled=True)]
    all_to_all x1, waiting for transfers between devices: 7.58 us -> 3.25 us  [kernel_body(): back = lax.all_to_all(spectra, 'ma', 0, 0, tiled=True)]
    convert_element_type x1, other arithmetic: 6.36 us -> 3.51 us  [kernel_body(): wave_low = (wave - rounded).astype(jnp.bfloat16)]
  transfers between devices with their start and end apart: 8 -> 9, of which waited for: 5 -> 4; matrix products, arithmetic and copies ran while one was open for 15% -> 17% of each run, Pallas kernels for 48% -> 12%
where the time goes in v2:
time: 219 us; the launch traced here: 218 us
  Pallas kernels  94.6 us (43%)
  other arithmetic  36.7 us (17%)
  waiting for transfers between devices  34.2 us (16%)
  starting transfers between devices  26.8 us (12%)
  blocking collectives  16.4 us (7%)
  local copies, waits for them, and re-layouts  8.72 us (4%)
    pallas_call x1, Pallas kernels, synthesis(): pl.pallas_call(functools.partial(synthesis_kernel, step_count=step_count)...  47.3 us
    pallas_call x1, Pallas kernels, analysis(): pl.pallas_call(functools.partial(analysis_kernel, step_count=step_count),...  26.6 us
    unnamed x11, other arithmetic  22 us
    pallas_call x1, Pallas kernels, grid_step(): pl.pallas_call(functools.partial(grid_kernel, step_count=step_count, slop...  20.6 us
    all_to_all x1, blocking collectives, kernel_body(): solved = lax.all_to_all(jnp.stack(solved[::-1]), 'row', 0, 0, tiled=True)  16.4 us
    all_to_all x1, waiting for transfers between devices, kernel_body(): shells = lax.all_to_all(right_side, 'row', 0, 0, tiled=True)  14.6 us
    ppermute x1, waiting for transfers between devices, kernel_body(): below = lax.ppermute(pair, 'row', forward)  12.3 us
    ppermute x3, starting transfers between devices, kernel_body(): lax.ppermute(small, 'row', [(i, (i + shift) % row_count) for i in range(r...  4.57 us
  transfers between devices with their start and end apart: 9, of which 4 were waited for; matrix products, arithmetic and copies ran while one was open for 17% of the time, Pallas kernels for 12%

profile of v2, /device:TPU:2, one launch (start us, length us, event | category | flops | bytes accessed | tf_op | source)
XLA Modules:
  0.0 218.4 jit_solution(7159741789083983200)
XLA Ops:
  4.7 47.3 %synthesis.1 = (f32[8,2,96,128]{3,2,1,0:T(8,128)}, f32[8,5,96,128]{3,2,1,0:T(8,128)}, bf16[64,512,384]{2,1,0:T(8,128)(2,1)}, bf16[64,512,384]{2,1,0:T(8,128)(2,1)}) custom-call(f32[2,1,64,512]{3,2,1,0:T(8,128)} %psi_ref.1, f32[2,1,64,512]{3,2,1,0:T(8,128)} %heat_ref.3, f32[2,1,64,512]{3,2,1,0:T(8,128)} %mag_ref.3, f32[2,1,64,512]{3,2,1,0:T(8,128)} %speed_ref.1, ...), custom_call_target="tpu_custom_call" | custom-call | flops 3623878656 | bytes 50331648 | tf_op jit(solution)/shard_map/synthesis/pallas_call | solution.py:481
  52.1 4.4 %all-to-all-start = ((f32[8,2,96,128]{3,2,1,0:T(8,128)}), f32[8,2,96,128]{3,2,1,0:T(8,128)}, u32[]{:S(2)}, u32[]{:S(2)}) async-start(f32[8,2,96,128]{3,2,1,0:T(8,128)} %get-tuple-element.10), calls=%async_computation | async-start | bytes 1572864 | tf_op jit(solution)/shard_map/all_to_all | solution.py:769
  61.1 2.0 subtract_dynamic-update-slice_fusion.11
  65.1 2.0 subtract_dynamic-update-slice_fusion.9
  67.1 2.0 subtract_dynamic-update-slice_fusion.8
  75.0 2.0 subtract_dynamic-update-slice_fusion.4
  77.0 2.0 subtract_dynamic-update-slice_fusion.3
  79.0 2.0 subtract_dynamic-update-slice_fusion.2
  81.1 2.0 subtract_dynamic-update-slice_fusion.1
  83.1 4.3 %all-to-all-start.1 = ((f32[8,5,96,128]{3,2,1,0:T(8,128)}), f32[8,5,96,128]{3,2,1,0:T(8,128)}, u32[]{:S(2)}, u32[]{:S(2)}) async-start(f32[8,5,96,128]{3,2,1,0:T(8,128)} %get-tuple-element.13), calls=%async_computation.1 | async-start | bytes 3932160 | tf_op jit(solution)/shard_map/all_to_all | solution.py:771
  87.4 2.0 subtract_dynamic-update-slice_fusion
  89.4 2.5 %pad_maximum_fusion = f32[8,2,64,1536]{3,2,1,0:T(8,128)S(1)} fusion(f32[8,1,64,1536]{3,2,1,0:T(8,128)} %get-tuple-element.69, f32[8,1,64,1536]{3,2,1,0:T(8,128)S(1)} %get-tuple-element.68), kind=kLoop, calls=%fused_computation.3 | loop fusion | flops 1572864 | bytes 12582912 | tf_op jit(solution)/shard_map/stack | solution.py:774
  91.9 4.0 %collective-permute-start.1 = (f32[8,2,96,128]{3,2,1,0:T(8,128)}, f32[8,2,96,128]{3,2,1,0:T(8,128)S(1)}, u32[]{:S(2)}, u32[]{:S(2)}) collective-permute-start(f32[8,2,96,128]{3,2,1,0:T(8,128)} %all-to-all-done.pair_ref), channel_id=1, source_target_pairs={{0,8},{8,16},{16,24},{1,9},{9,17},{17,25},{2,10},{10,18},{18,26},{... | collective-permute-start | bytes 2359304 | tf_op jit(solution)/shard_map/ppermute | solution.py:787
  97.5 3.5 %fusion = (bf16[1024,1536]{1,0:T(8,128)(2,1)}, bf16[1024,1536]{1,0:T(8,128)(2,1)}) fusion(f32[8,2,64,1536]{3,2,1,0:T(8,128)S(1)} %pad_maximum_fusion), kind=kLoop, calls=%fused_computation.2 | loop fusion | flops 6291456 | bytes 12582912 | tf_op jit(solution)/shard_map/convert_element_type | solution.py:779
  101.0 12.3 %collective-permute-done.1.below_ref = f32[8,2,96,128]{3,2,1,0:T(8,128)S(1)} collective-permute-done((f32[8,2,96,128]{3,2,1,0:T(8,128)}, f32[8,2,96,128]{3,2,1,0:T(8,128)S(1)}, u32[]{:S(2)}, u32[]{:S(2)}) %collective-permute-start.1) | collective-permute-done | bytes 786464 | tf_op jit(solution)/shard_map/ppermute | solution.py:787
  113.3 4.1 %collective-permute-done.above_ref = f32[8,2,96,128]{3,2,1,0:T(8,128)S(1)} collective-permute-done((f32[8,2,96,128]{3,2,1,0:T(8,128)}, f32[8,2,96,128]{3,2,1,0:T(8,128)S(1)}, u32[]{:S(2)}, u32[]{:S(2)}) %collective-permute-start) | collective-permute-done | bytes 786464 | tf_op jit(solution)/shard_map/ppermute | solution.py:788
  118.3 20.6 %grid_step.1 = f32[8,2,96,128]{3,2,1,0:T(8,128)} custom-call(f32[8,2,96,128]{3,2,1,0:T(8,128)} %all-to-all-done.pair_ref, f32[8,5,96,128]{3,2,1,0:T(8,128)} %all-to-all-done.1.rest_ref, f32[8,2,96,128]{3,2,1,0:T(8,128)} %copy-done.6, f32[8,2,96,128]{3,2,1,0:T(8,128)} %copy-done.5, f32[1,1024]{1,0:T(1,128)} %reshape.1236.weight_ref, ...), custom_call_target="tpu_custom_call" | custom-call | flops 9965666304 | bytes 6291456 | tf_op jit(solution)/shard_map/grid_step/pallas_call | solution.py:574
  138.9 4.2 %all-to-all-start.2 = ((f32[8,2,96,128]{3,2,1,0:T(8,128)}), f32[8,2,96,128]{3,2,1,0:T(8,128)S(1)}, u32[]{:S(2)}, u32[]{:S(2)}) async-start(f32[8,2,96,128]{3,2,1,0:T(8,128)} %grid_step.1), calls=%async_computation.2 | async-start | bytes 1572864 | tf_op jit(solution)/shard_map/all_to_all | solution.py:811
  143.1 2.7 %fusion.7 = f32[384]{0:T(512)S(1)} fusion(f32[384]{0:T(512)S(1)} %fusion.57, s32[384]{0:T(512)S(1)} %get-tuple-element.109, s32[384]{0:T(512)S(1)} %get-tuple-element.110), kind=kLoop, calls=%fused_computation.12 | loop fusion | flops 1621632 | bytes 6144 | tf_op jit(solution)/shard_map/reduce_sum | solution.py:161
  151.0 3.2 %all-to-all-done.2.back_ref = f32[8,2,96,128]{3,2,1,0:T(8,128)S(1)} async-done(((f32[8,2,96,128]{3,2,1,0:T(8,128)}), f32[8,2,96,128]{3,2,1,0:T(8,128)S(1)}, u32[]{:S(2)}, u32[]{:S(2)}) %all-to-all-start.2) | async-done | bytes 786464 | tf_op jit(solution)/shard_map/all_to_all | solution.py:811
  155.1 26.6 %analysis.1 = f32[4,2,2,16,512]{4,3,2,1,0:T(8,128)} custom-call(f32[8,2,96,128]{3,2,1,0:T(8,128)} %copy-done, f32[1,384]{1,0:T(1,128)} %mul.1425.quad_ref, f32[64,512]{1,0:T(8,128)} %fusion.33.sign_ref, f32[2,1,64,512]{3,2,1,0:T(8,128)} %heat_ref.3, f32[2,1,64,512]{3,2,1,0:T(8,128)} %mag_ref.3, bf16[64,512,384]{2,1,0:T(8,128)(2,1)} %get-tuple-element.15.high_ref, ...), custom_call_target="tpu_custom_call" | custom-call | flops 603979776 | bytes 50331648 | tf_op jit(solution)/shard_map/analysis/pallas_call | solution.py:666
  181.7 3.8 %all-to-all-start.3 = ((f32[4,2,2,16,512]{4,3,2,1,0:T(8,128)}), f32[4,2,2,16,512]{4,3,2,1,0:T(8,128)S(1)}, u32[]{:S(2)}, u32[]{:S(2)}) async-start(f32[4,2,2,16,512]{4,3,2,1,0:T(8,128)} %analysis.1), calls=%async_computation.3 | async-start | bytes 1048576 | tf_op jit(solution)/shard_map/all_to_all | solution.py:817
  185.7 14.6 %all-to-all-done.3 = f32[4,2,2,16,512]{4,3,2,1,0:T(8,128)S(1)} async-done(((f32[4,2,2,16,512]{4,3,2,1,0:T(8,128)}), f32[4,2,2,16,512]{4,3,2,1,0:T(8,128)S(1)}, u32[]{:S(2)}, u32[]{:S(2)}) %all-to-all-start.3) | async-done | bytes 524320 | tf_op jit(solution)/shard_map/all_to_all | solution.py:817
  200.4 16.4 %all_to_all.25 = f32[4,2,2,16,512]{4,3,2,1,0:T(8,128)S(1)} all-to-all(f32[4,2,2,16,512]{4,3,2,1,0:T(8,128)S(1)} %pad_maximum_fusion.1), channel_id=1, replica_groups=mesh['row'=4,'ma'=8] {'row'}, dimensions={0} | all-to-all | bytes 1048576 | tf_op jit(solution)/shard_map/all_to_all | solution.py:829
  (95 shorter events, 26.8 us)
Async XLA Ops:
  4.7 51.7 %copy-start.1 = (s32[512]{0:T(512)S(1)}, s32[512]{0:T(512)}, u32[]{:S(2)}) copy-start(s32[512]{0:T(512)} %param.12) | copy-start | bytes 6148
  52.1 31.0 %all-to-all-start = ((f32[8,2,96,128]{3,2,1,0:T(8,128)}), f32[8,2,96,128]{3,2,1,0:T(8,128)}, u32[]{:S(2)}, u32[]{:S(2)}) async-start(f32[8,2,96,128]{3,2,1,0:T(8,128)} %get-tuple-element.10), calls=%async_computation | async-start | bytes 1572864 | tf_op jit(solution)/shard_map/all_to_all | solution.py:769
  75.0 12.4 %copy-start.2 = (f32[2,1,512]{2,1,0:T(1,128)S(1)}, f32[2,1,512]{2,1,0:T(1,128)}, u32[]{:S(2)}) copy-start(f32[2,1,512]{2,1,0:T(1,128)} %param.15) | copy-start | bytes 12292
  75.0 12.4 %copy-start.3 = (f32[2,1,512]{2,1,0:T(1,128)S(1)}, f32[2,1,512]{2,1,0:T(1,128)}, u32[]{:S(2)}) copy-start(f32[2,1,512]{2,1,0:T(1,128)} %param.14) | copy-start | bytes 12292
  75.0 12.4 %copy-start.4 = (f32[2,1,512]{2,1,0:T(1,128)S(1)}, f32[2,1,512]{2,1,0:T(1,128)}, u32[]{:S(2)}) copy-start(f32[2,1,512]{2,1,0:T(1,128)} %param.13) | copy-start | bytes 12292
  83.1 34.3 %all-to-all-start.1 = ((f32[8,5,96,128]{3,2,1,0:T(8,128)}), f32[8,5,96,128]{3,2,1,0:T(8,128)}, u32[]{:S(2)}, u32[]{:S(2)}) async-start(f32[8,5,96,128]{3,2,1,0:T(8,128)} %get-tuple-element.13), calls=%async_computation.1 | async-start | bytes 3932160 | tf_op jit(solution)/shard_map/all_to_all | solution.py:771
  91.9 21.4 %collective-permute-start.1 = (f32[8,2,96,128]{3,2,1,0:T(8,128)}, f32[8,2,96,128]{3,2,1,0:T(8,128)S(1)}, u32[]{:S(2)}, u32[]{:S(2)}) collective-permute-start(f32[8,2,96,128]{3,2,1,0:T(8,128)} %all-to-all-done.pair_ref), channel_id=1, source_target_pairs={{0,8},{8,16},{16,24},{1,9},{9,17},{17,25},{2,10},{10,18},{18,26},{... | collective-permute-start | bytes 2359304 | tf_op jit(solution)/shard_map/ppermute | solution.py:787
  96.0 21.4 %collective-permute-start = (f32[8,2,96,128]{3,2,1,0:T(8,128)}, f32[8,2,96,128]{3,2,1,0:T(8,128)S(1)}, u32[]{:S(2)}, u32[]{:S(2)}) collective-permute-start(f32[8,2,96,128]{3,2,1,0:T(8,128)} %all-to-all-done.pair_ref), channel_id=1, source_target_pairs={{8,0},{16,8},{24,16},{9,1},{17,9},{25,17},{10,2},{18,10},{26,18},{... | collective-permute-start | bytes 2359304 | tf_op jit(solution)/shard_map/ppermute | solution.py:788
  113.3 4.1 %copy-start.5 = (f32[8,2,96,128]{3,2,1,0:T(8,128)}, f32[8,2,96,128]{3,2,1,0:T(8,128)S(1)}, u32[]{:S(2)}) copy-start(f32[8,2,96,128]{3,2,1,0:T(8,128)S(1)} %collective-permute-done.1.below_ref) | copy-start | bytes 2359300
  117.4 0.9 copy-start.6
  138.9 15.3 %all-to-all-start.2 = ((f32[8,2,96,128]{3,2,1,0:T(8,128)}), f32[8,2,96,128]{3,2,1,0:T(8,128)S(1)}, u32[]{:S(2)}, u32[]{:S(2)}) async-start(f32[8,2,96,128]{3,2,1,0:T(8,128)} %grid_step.1), calls=%async_computation.2 | async-start | bytes 1572864 | tf_op jit(solution)/shard_map/all_to_all | solution.py:811
  146.3 39.3 %collective-permute-start.4 = (f32[3,2,1,512]{3,2,1,0:T(1,128)S(1)}, f32[3,2,1,512]{3,2,1,0:T(1,128)S(1)}, u32[]{:S(2)}, u32[]{:S(2)}) collective-permute-start(f32[3,2,1,512]{3,2,1,0:T(1,128)S(1)} %pad_maximum_fusion.2), channel_id=1, source_target_pairs={{0,24},{8,0},{16,8},{24,16},{1,25},{9,1},{17,9},{25,17},{2,26},{10... | collective-permute-start | bytes 36872 | tf_op jit(solution)/shard_map/ppermute | solution.py:803
  148.0 37.6 %collective-permute-start.3 = (f32[3,2,1,512]{3,2,1,0:T(1,128)S(1)}, f32[3,2,1,512]{3,2,1,0:T(1,128)S(1)}, u32[]{:S(2)}, u32[]{:S(2)}) collective-permute-start(f32[3,2,1,512]{3,2,1,0:T(1,128)S(1)} %pad_maximum_fusion.2), channel_id=1, source_target_pairs={{0,16},{8,24},{16,0},{24,8},{1,17},{9,25},{17,1},{25,9},{2,18},{10... | collective-permute-start | bytes 36872 | tf_op jit(solution)/shard_map/ppermute | solution.py:803
  149.3 36.2 %collective-permute-start.2 = (f32[3,2,1,512]{3,2,1,0:T(1,128)S(1)}, f32[3,2,1,512]{3,2,1,0:T(1,128)S(1)}, u32[]{:S(2)}, u32[]{:S(2)}) collective-permute-start(f32[3,2,1,512]{3,2,1,0:T(1,128)S(1)} %pad_maximum_fusion.2), channel_id=1, source_target_pairs={{0,8},{8,16},{16,24},{24,0},{1,9},{9,17},{17,25},{25,1},{2,10},{10... | collective-permute-start | bytes 36872 | tf_op jit(solution)/shard_map/ppermute | solution.py:803
  154.2 0.9 copy-start
  181.7 18.5 %all-to-all-start.3 = ((f32[4,2,2,16,512]{4,3,2,1,0:T(8,128)}), f32[4,2,2,16,512]{4,3,2,1,0:T(8,128)S(1)}, u32[]{:S(2)}, u32[]{:S(2)}) async-start(f32[4,2,2,16,512]{4,3,2,1,0:T(8,128)} %analysis.1), calls=%async_computation.3 | async-start | bytes 1048576 | tf_op jit(solution)/shard_map/all_to_all | solution.py:817

commit v3 on v2

--- a/solution.py
+++ b/solution.py
@@ -517,7 +517,7 @@
 
 
 def grid_kernel(
-    pair_ref, rest_ref, above_ref, below_ref, weight_ref, spin_ref, high_ref, low_ref, factor_ref,
+    pair_ref, rest_ref, above_ref, below_ref, weight_ref, spin_ref, near_ref, far_ref, factor_ref,
     out_ref, sets, total, *, step_count, slope_scale, lon_total,
 ):
     step = pl.program_id(0)
@@ -545,15 +545,21 @@
                 sets[q * rows : (q + 1) * rows, cut] = high
                 sets[count + q * rows : count + (q + 1) * rows, cut] = low
 
-    both = dot(sets[...], high_ref[...])
-    grids = both[:count] + both[count:] + dot(sets[:count], low_ref[...])
+    pieces = [
+        far_ref[0, :, 2 * a : 2 * a + 1] * near_ref[0]
+        + far_ref[0, :, 2 * a + 1 : 2 * a + 2] * near_ref[1]
+        for a in range(far_ref.shape[2] // 2)
+    ]
+    wave_high, wave_low = halves(jnp.concatenate(pieces, axis=1))
+    both = dot(sets[...], wave_high)
+    grids = both[:count] + both[count:] + dot(sets[:count], wave_low)
     g = [grids[q * rows : (q + 1) * rows] for q in range(9)]
     factor = factor_ref[...]
     heat = -((g[3] * g[1] - g[0] * g[4]) * factor + g[6] * g[7])
     induction = -((g[3] * g[2] - g[0] * g[5]) * factor + g[6] * g[8])
     high, low = halves(jnp.concatenate([heat, induction], axis=0))
-    back = dot_t(jnp.concatenate([high, low], axis=0), high_ref[...])
-    total[...] += back[: 2 * rows] + back[2 * rows :] + dot_t(high, low_ref[...])
+    back = dot_t(jnp.concatenate([high, low], axis=0), wave_high)
+    total[...] += back[: 2 * rows] + back[2 * rows :] + dot_t(high, wave_low)
 
     @pl.when(step == step_count - 1)
     def _():
@@ -563,13 +569,11 @@
                 out_ref[source, f] = total[f * rows : (f + 1) * rows, cut] * (1.0 / lon_total)
 
 
-def grid_step(pair, rest, above, below, weight, spin, wave_high, wave_low, factor, slope_scale):
+def grid_step(pair, rest, above, below, weight, spin, near, far, factor, slope_scale, lon_total):
     sources, _, rows, lanes = pair.shape
-    waves, lon_total = wave_high.shape
-    lon_block = math.gcd(256, lon_total)
-    step_count = lon_total // lon_block
+    step_count, waves, _ = far.shape
     whole = lambda shape: pl.BlockSpec(shape, lambda i: (0,) * len(shape))
-    wave_spec = pl.BlockSpec((waves, lon_block), lambda i: (0, i))
+    far_spec = pl.BlockSpec((1, waves, far.shape[2]), lambda i: (i, 0, 0))
     out_shape = (sources, 2, rows, lanes)
     return pl.pallas_call(
         functools.partial(
@@ -578,7 +582,7 @@
         grid=(step_count,),
         in_specs=[
             whole(pair.shape), whole(rest.shape), whole(above.shape), whole(below.shape),
-            whole(weight.shape), whole(spin.shape), wave_spec, wave_spec, whole(factor.shape),
+            whole(weight.shape), whole(spin.shape), whole(near.shape), far_spec, whole(factor.shape),
         ],
         out_specs=whole(out_shape),
         out_shape=jax.ShapeDtypeStruct(out_shape, jnp.float32),
@@ -593,7 +597,7 @@
             transcendentals=0,
         ),
         name="grid_step",
-    )(pair, rest, above, below, weight, spin, wave_high, wave_low, factor)
+    )(pair, rest, above, below, weight, spin, near, far, factor)
 
 
 def analysis_kernel(
@@ -688,21 +692,17 @@
     )(back, quad, sign, heat, mag, high, low)
 
 
-def wave_halves(orders, lon_total):
+def wave_factors(orders, lon_total):
     width = 128
+
     def pair(columns):
         phase_int = orders[:, None] * columns[None, :] % lon_total
         angle_vals = 2.0 * math.pi / lon_total * phase_int.astype(jnp.float32)
         return jnp.cos(angle_vals), jnp.sin(angle_vals)
 
-    fine_cos, fine_sin = pair(jnp.arange(width, dtype=jnp.int32))
-    far_cos, far_sin = pair(jnp.arange(lon_total // width, dtype=jnp.int32) * width)
-    cos_parts, sin_parts = [], []
-    for a in range(lon_total // width):
-        ca, sa = far_cos[:, a : a + 1], far_sin[:, a : a + 1]
-        cos_parts.append(ca * fine_cos - sa * fine_sin)
-        sin_parts.append(-(sa * fine_cos + ca * fine_sin))
-    return jnp.concatenate(cos_parts, axis=1), jnp.concatenate(sin_parts, axis=1)
+    near = pair(jnp.arange(width, dtype=jnp.int32))
+    far = pair(jnp.arange(lon_total // width, dtype=jnp.int32) * width)
+    return near, far
 
 
 def kernel_body(
@@ -770,13 +770,16 @@
     pair, rest = lax.optimization_barrier((pair, rest))
     rest = lax.all_to_all(rest, "ma", 0, 0, tiled=True)
 
-    cos_wave, sin_wave = wave_halves(position_azimuth_map, NLON)
-    wave = jnp.stack(
-        [cos_wave.reshape(ma_count, local, NLON), sin_wave.reshape(ma_count, local, NLON)], axis=1
-    ).reshape(2 * ma_count * local, NLON)
-    rounded = lax.reduce_precision(wave, 8, 7)
-    wave_high = rounded.astype(jnp.bfloat16)
-    wave_low = (wave - rounded).astype(jnp.bfloat16)
+    (near_cos, near_sin), (far_cos, far_sin) = wave_factors(position_azimuth_map, NLON)
+    chunk = math.gcd(2, far_cos.shape[1])
+
+    def by_component(first, second):
+        parts = [v.reshape(ma_count, local, v.shape[1]) for v in (first, second)]
+        return jnp.stack(parts, axis=1).reshape(2 * ma_count * local, first.shape[1])
+
+    near = jnp.stack([by_component(near_cos, near_cos), by_component(near_sin, near_sin)])
+    far = jnp.stack([by_component(far_cos, -far_sin), by_component(-far_sin, -far_cos)], axis=2)
+    far = jnp.moveaxis(far.reshape(far.shape[0], -1, 2 * chunk), 1, 0)
     orders = position_azimuth_map.astype(jnp.float32).reshape(ma_count, 1, local)
     weight = jnp.where(orders == 0.0, 1.0, 2.0)
     spin = jnp.concatenate([-orders * weight, orders * weight], axis=1).reshape(1, -1)
@@ -793,7 +796,7 @@
     factor = 1.0 / (radius * radius * (sine_mine * sine_mine))
     factor = jnp.concatenate([factor, factor])[:, None]
     spectra = grid_step(
-        pair, rest, above, below, weight, spin, wave_high, wave_low, factor, 1.0 / (2.0 * spacing)
+        pair, rest, above, below, weight, spin, near, far, factor, 1.0 / (2.0 * spacing), NLON
     )
     small = jnp.stack([subdiagonal_complement, superdiagonal_complement, diagonal_entries])
     small, spectra = lax.optimization_barrier((small, spectra))

time: 219 us -> 202 us (0.922)
  other arithmetic: 36.7 us -> 9.09 us
  starting transfers between devices: 26.8 us -> 32.5 us
  waiting for transfers between devices: 34.2 us -> 37 us
    unnamed x11 -> x0, other arithmetic: 22 us -> none
    ppermute x1, waiting for transfers between devices: 12.3 us -> 1.08 us  [kernel_body(): below = lax.ppermute(pair, 'row', forward)]
    all_to_all x1, waiting for transfers between devices: 0.01 us -> 10.9 us  [kernel_body(): pair = lax.all_to_all(pair, 'ma', 0, 0, tiled=True)]
    ppermute x1, waiting for transfers between devices: 4.05 us -> 7.96 us  [kernel_body(): above = lax.ppermute(pair, 'row', backward)]
    convert_element_type x1 -> x0, other arithmetic: 3.51 us -> none  [kernel_body(): wave_low = (wave - rounded).astype(jnp.bfloat16)]
    reshape x0 -> x2, local copies, waits for them, and re-layouts: none -> 2.28 us  [kernel_body(): far = jnp.moveaxis(far.reshape(far.shape[0], -1, 2 * chunk), 1, 0)]
  transfers between devices with their start and end apart: 9 -> 9, of which waited for: 4 -> 6; matrix products, arithmetic and copies ran while one was open for 17% -> 6% of each run, Pallas kernels for 12% -> 13%
where the time goes in v3:
time: 202 us
  Pallas kernels  96.1 us (48%)
  waiting for transfers between devices  37 us (18%)
  starting transfers between devices  32.5 us (16%)
  blocking collectives  16.4 us (8%)
  local copies, waits for them, and re-layouts  9.93 us (5%)
  other arithmetic  9.09 us (4%)
    pallas_call x1, Pallas kernels, synthesis(): pl.pallas_call(functools.partial(synthesis_kernel, step_count=step_count)...  47.3 us
    pallas_call x1, Pallas kernels, analysis(): pl.pallas_call(functools.partial(analysis_kernel, step_count=step_count),...  26.6 us
    pallas_call x1, Pallas kernels, grid_step(): pl.pallas_call(functools.partial(grid_kernel, step_count=step_count, slop...  22.1 us
    all_to_all x1, blocking collectives, kernel_body(): solved = lax.all_to_all(jnp.stack(solved[::-1]), 'row', 0, 0, tiled=True)  16.4 us
    all_to_all x1, waiting for transfers between devices, kernel_body(): shells = lax.all_to_all(right_side, 'row', 0, 0, tiled=True)  14.6 us
    all_to_all x1, waiting for transfers between devices, kernel_body(): pair = lax.all_to_all(pair, 'ma', 0, 0, tiled=True)  10.9 us
    ppermute x1, waiting for transfers between devices, kernel_body(): above = lax.ppermute(pair, 'row', backward)  7.96 us
    all_to_all x1, starting transfers between devices, kernel_body(): shells = lax.all_to_all(right_side, 'row', 0, 0, tiled=True)  5.82 us
  transfers between devices with their start and end apart: 9, of which 6 were waited for; matrix products, arithmetic and copies ran while one was open for 6% of the time, Pallas kernels for 13%

profile of v3, /device:TPU:2, one launch (start us, length us, event | category | flops | bytes accessed | tf_op | source)
XLA Modules:
  0.0 201.9 jit_solution(15122658339854266894)
XLA Ops:
  3.7 1.0 fusion.21
  4.8 47.3 %synthesis.1 = (f32[8,2,96,128]{3,2,1,0:T(8,128)}, f32[8,5,96,128]{3,2,1,0:T(8,128)}, bf16[64,512,384]{2,1,0:T(8,128)(2,1)}, bf16[64,512,384]{2,1,0:T(8,128)(2,1)}) custom-call(f32[2,1,64,512]{3,2,1,0:T(8,128)} %psi_ref.1, f32[2,1,64,512]{3,2,1,0:T(8,128)} %heat_ref.3, f32[2,1,64,512]{3,2,1,0:T(8,128)} %mag_ref.3, f32[2,1,64,512]{3,2,1,0:T(8,128)} %speed_ref.1, ...), custom_call_target="tpu_custom_call" | custom-call | flops 3623878656 | bytes 50331648 | tf_op jit(solution)/shard_map/synthesis/pallas_call | solution.py:481
  52.1 4.3 %all-to-all-start = ((f32[8,2,96,128]{3,2,1,0:T(8,128)}), f32[8,2,96,128]{3,2,1,0:T(8,128)S(1)}, u32[]{:S(2)}, u32[]{:S(2)}) async-start(f32[8,2,96,128]{3,2,1,0:T(8,128)} %get-tuple-element.10), calls=%async_computation | async-start | bytes 1572864 | tf_op jit(solution)/shard_map/all_to_all | solution.py:769
  56.5 10.9 %all-to-all-done.pair_ref = f32[8,2,96,128]{3,2,1,0:T(8,128)S(1)} async-done(((f32[8,2,96,128]{3,2,1,0:T(8,128)}), f32[8,2,96,128]{3,2,1,0:T(8,128)S(1)}, u32[]{:S(2)}, u32[]{:S(2)}) %all-to-all-start) | async-done | bytes 786464 | tf_op jit(solution)/shard_map/all_to_all | solution.py:769
  67.5 5.0 %all-to-all-start.1 = ((f32[8,5,96,128]{3,2,1,0:T(8,128)}), f32[8,5,96,128]{3,2,1,0:T(8,128)S(1)}, u32[]{:S(2)}, u32[]{:S(2)}) async-start(f32[8,5,96,128]{3,2,1,0:T(8,128)} %get-tuple-element.13), calls=%async_computation.1 | async-start | bytes 3932160 | tf_op jit(solution)/shard_map/all_to_all | solution.py:771
  73.4 1.3 collective-permute-start
  74.7 5.5 %collective-permute-start.1 = (f32[8,2,96,128]{3,2,1,0:T(8,128)S(1)}, f32[8,2,96,128]{3,2,1,0:T(8,128)}, u32[]{:S(2)}, u32[]{:S(2)}) collective-permute-start(f32[8,2,96,128]{3,2,1,0:T(8,128)S(1)} %all-to-all-done.pair_ref), channel_id=1, source_target_pairs={{0,8},{8,16},{16,24},{1,9},{9,17},{17,25},{2,10},{10,18},{18,26},{... | collective-permute-start | bytes 2359304 | tf_op jit(solution)/shard_map/ppermute | solution.py:790
  81.8 2.2 %copy.48 = f32[1024,6,4]{2,0,1:T(8,128)} copy(f32[1024,6,4]{0,2,1:T(4,128)S(1)} %reshape.501) | data formatting | bytes 196608 | tf_op jit(solution)/shard_map/reshape | solution.py:782
  84.7 1.1 fusion.13
  86.0 1.0 pad_maximum_fusion.near_ref
  87.0 8.0 %collective-permute-done.above_ref = f32[8,2,96,128]{3,2,1,0:T(8,128)} collective-permute-done((f32[8,2,96,128]{3,2,1,0:T(8,128)S(1)}, f32[8,2,96,128]{3,2,1,0:T(8,128)}, u32[]{:S(2)}, u32[]{:S(2)}) %collective-permute-start) | collective-permute-done | bytes 786464 | tf_op jit(solution)/shard_map/ppermute | solution.py:791
  95.0 1.1 collective-permute-done.1.below_ref
  96.2 1.3 copy-done.1
  97.5 22.1 %grid_step.1 = f32[8,2,96,128]{3,2,1,0:T(8,128)} custom-call(f32[8,2,96,128]{3,2,1,0:T(8,128)} %copy-done.2, f32[8,5,96,128]{3,2,1,0:T(8,128)} %copy-done.1, f32[8,2,96,128]{3,2,1,0:T(8,128)} %collective-permute-done.above_ref, f32[8,2,96,128]{3,2,1,0:T(8,128)} %collective-permute-done.1.below_ref, f32[1,1024]{1,0:T(1,128)} %reshape.499.weight_ref, ...), custom_call_target="tpu_custom_call" | custom-call | flops 9965666304 | bytes 6291456 | tf_op jit(solution)/shard_map/grid_step/pallas_call | solution.py:578
  119.6 5.0 %all-to-all-start.2 = ((f32[8,2,96,128]{3,2,1,0:T(8,128)}), f32[8,2,96,128]{3,2,1,0:T(8,128)S(1)}, u32[]{:S(2)}, u32[]{:S(2)}) async-start(f32[8,2,96,128]{3,2,1,0:T(8,128)} %grid_step.1), calls=%async_computation.2 | async-start | bytes 1572864 | tf_op jit(solution)/shard_map/all_to_all | solution.py:814
  124.6 2.7 %fusion.6 = f32[384]{0:T(512)S(1)} fusion(f32[384]{0:T(512)S(1)} %fusion.56, s32[384]{0:T(512)S(1)} %get-tuple-element.70, s32[384]{0:T(512)S(1)} %get-tuple-element.71), kind=kLoop, calls=%fused_computation.9 | loop fusion | flops 1621632 | bytes 6144 | tf_op jit(solution)/shard_map/reduce_sum | solution.py:161
  127.8 1.7 collective-permute-start.2
  129.5 3.5 %collective-permute-start.3 = (f32[3,2,1,512]{3,2,1,0:T(1,128)S(1)}, f32[3,2,1,512]{3,2,1,0:T(1,128)S(1)}, u32[]{:S(2)}, u32[]{:S(2)}) collective-permute-start(f32[3,2,1,512]{3,2,1,0:T(1,128)S(1)} %pad_maximum_fusion.7), channel_id=1, source_target_pairs={{0,16},{8,24},{16,0},{24,8},{1,17},{9,25},{17,1},{25,9},{2,18},{10... | collective-permute-start | bytes 36872 | tf_op jit(solution)/shard_map/ppermute | solution.py:806
  133.5 2.2 %all-to-all-done.2.back_ref = f32[8,2,96,128]{3,2,1,0:T(8,128)S(1)} async-done(((f32[8,2,96,128]{3,2,1,0:T(8,128)}), f32[8,2,96,128]{3,2,1,0:T(8,128)S(1)}, u32[]{:S(2)}, u32[]{:S(2)}) %all-to-all-start.2) | async-done | bytes 786464 | tf_op jit(solution)/shard_map/all_to_all | solution.py:814
  135.7 0.9 copy-done
  136.6 26.6 %analysis.1 = f32[4,2,2,16,512]{4,3,2,1,0:T(8,128)} custom-call(f32[8,2,96,128]{3,2,1,0:T(8,128)} %copy-done, f32[1,384]{1,0:T(1,128)} %mul.463.quad_ref, f32[64,512]{1,0:T(8,128)} %fusion.32.sign_ref, f32[2,1,64,512]{3,2,1,0:T(8,128)} %heat_ref.3, f32[2,1,64,512]{3,2,1,0:T(8,128)} %mag_ref.3, bf16[64,512,384]{2,1,0:T(8,128)(2,1)} %get-tuple-element.15.high_ref, ...), custom_call_target="tpu_custom_call" | custom-call | flops 603979776 | bytes 50331648 | tf_op jit(solution)/shard_map/analysis/pallas_call | solution.py:670
  163.2 5.8 %all-to-all-start.3 = ((f32[4,2,2,16,512]{4,3,2,1,0:T(8,128)}), f32[4,2,2,16,512]{4,3,2,1,0:T(8,128)S(1)}, u32[]{:S(2)}, u32[]{:S(2)}) async-start(f32[4,2,2,16,512]{4,3,2,1,0:T(8,128)} %analysis.1), calls=%async_computation.3 | async-start | bytes 1048576 | tf_op jit(solution)/shard_map/all_to_all | solution.py:820
  169.2 14.6 %all-to-all-done.3 = f32[4,2,2,16,512]{4,3,2,1,0:T(8,128)S(1)} async-done(((f32[4,2,2,16,512]{4,3,2,1,0:T(8,128)}), f32[4,2,2,16,512]{4,3,2,1,0:T(8,128)S(1)}, u32[]{:S(2)}, u32[]{:S(2)}) %all-to-all-start.3) | async-done | bytes 524320 | tf_op jit(solution)/shard_map/all_to_all | solution.py:820
  184.0 16.4 %all_to_all.25 = f32[4,2,2,16,512]{4,3,2,1,0:T(8,128)S(1)} all-to-all(f32[4,2,2,16,512]{4,3,2,1,0:T(8,128)S(1)} %pad_maximum_fusion.3), channel_id=1, replica_groups=mesh['row'=4,'ma'=8] {'row'}, dimensions={0} | all-to-all | bytes 1048576 | tf_op jit(solution)/shard_map/all_to_all | solution.py:832
  (67 shorter events, 9.5 us)
Async XLA Ops:
  4.8 51.6 %copy-start.3 = (s32[512]{0:T(512)S(1)}, s32[512]{0:T(512)}, u32[]{:S(2)}) copy-start(s32[512]{0:T(512)} %param.12) | copy-start | bytes 6148
  52.1 15.4 %all-to-all-start = ((f32[8,2,96,128]{3,2,1,0:T(8,128)}), f32[8,2,96,128]{3,2,1,0:T(8,128)S(1)}, u32[]{:S(2)}, u32[]{:S(2)}) async-start(f32[8,2,96,128]{3,2,1,0:T(8,128)} %get-tuple-element.10), calls=%async_computation | async-start | bytes 1572864 | tf_op jit(solution)/shard_map/all_to_all | solution.py:769
  67.5 16.5 %copy-start.2 = (f32[8,2,96,128]{3,2,1,0:T(8,128)}, f32[8,2,96,128]{3,2,1,0:T(8,128)S(1)}, u32[]{:S(2)}) copy-start(f32[8,2,96,128]{3,2,1,0:T(8,128)S(1)} %all-to-all-done.pair_ref) | copy-start | bytes 2359300
  67.5 28.8 %all-to-all-start.1 = ((f32[8,5,96,128]{3,2,1,0:T(8,128)}), f32[8,5,96,128]{3,2,1,0:T(8,128)S(1)}, u32[]{:S(2)}, u32[]{:S(2)}) async-start(f32[8,5,96,128]{3,2,1,0:T(8,128)} %get-tuple-element.13), calls=%async_computation.1 | async-start | bytes 3932160 | tf_op jit(solution)/shard_map/all_to_all | solution.py:771
  72.5 12.2 %copy-start.4 = (f32[2,1,512]{2,1,0:T(1,128)S(1)}, f32[2,1,512]{2,1,0:T(1,128)}, u32[]{:S(2)}) copy-start(f32[2,1,512]{2,1,0:T(1,128)} %param.15) | copy-start | bytes 12292
  72.5 12.2 %copy-start.5 = (f32[2,1,512]{2,1,0:T(1,128)S(1)}, f32[2,1,512]{2,1,0:T(1,128)}, u32[]{:S(2)}) copy-start(f32[2,1,512]{2,1,0:T(1,128)} %param.14) | copy-start | bytes 12292
  72.5 12.2 %copy-start.6 = (f32[2,1,512]{2,1,0:T(1,128)S(1)}, f32[2,1,512]{2,1,0:T(1,128)}, u32[]{:S(2)}) copy-start(f32[2,1,512]{2,1,0:T(1,128)} %param.13) | copy-start | bytes 12292
  73.4 21.6 %collective-permute-start = (f32[8,2,96,128]{3,2,1,0:T(8,128)S(1)}, f32[8,2,96,128]{3,2,1,0:T(8,128)}, u32[]{:S(2)}, u32[]{:S(2)}) collective-permute-start(f32[8,2,96,128]{3,2,1,0:T(8,128)S(1)} %all-to-all-done.pair_ref), channel_id=1, source_target_pairs={{8,0},{16,8},{24,16},{9,1},{17,9},{25,17},{10,2},{18,10},{26,18},{... | collective-permute-start | bytes 2359304 | tf_op jit(solution)/shard_map/ppermute | solution.py:791
  74.7 21.4 %collective-permute-start.1 = (f32[8,2,96,128]{3,2,1,0:T(8,128)S(1)}, f32[8,2,96,128]{3,2,1,0:T(8,128)}, u32[]{:S(2)}, u32[]{:S(2)}) collective-permute-start(f32[8,2,96,128]{3,2,1,0:T(8,128)S(1)} %all-to-all-done.pair_ref), channel_id=1, source_target_pairs={{0,8},{8,16},{16,24},{1,9},{9,17},{17,25},{2,10},{10,18},{18,26},{... | collective-permute-start | bytes 2359304 | tf_op jit(solution)/shard_map/ppermute | solution.py:790
  96.2 1.3 copy-start.1
  119.6 16.1 %all-to-all-start.2 = ((f32[8,2,96,128]{3,2,1,0:T(8,128)}), f32[8,2,96,128]{3,2,1,0:T(8,128)S(1)}, u32[]{:S(2)}, u32[]{:S(2)}) async-start(f32[8,2,96,128]{3,2,1,0:T(8,128)} %grid_step.1), calls=%async_computation.2 | async-start | bytes 1572864 | tf_op jit(solution)/shard_map/all_to_all | solution.py:814
  127.8 41.2 %collective-permute-start.2 = (f32[3,2,1,512]{3,2,1,0:T(1,128)S(1)}, f32[3,2,1,512]{3,2,1,0:T(1,128)S(1)}, u32[]{:S(2)}, u32[]{:S(2)}) collective-permute-start(f32[3,2,1,512]{3,2,1,0:T(1,128)S(1)} %pad_maximum_fusion.7), channel_id=1, source_target_pairs={{0,8},{8,16},{16,24},{24,0},{1,9},{9,17},{17,25},{25,1},{2,10},{10... | collective-permute-start | bytes 36872 | tf_op jit(solution)/shard_map/ppermute | solution.py:806
  129.5 39.6 %collective-permute-start.3 = (f32[3,2,1,512]{3,2,1,0:T(1,128)S(1)}, f32[3,2,1,512]{3,2,1,0:T(1,128)S(1)}, u32[]{:S(2)}, u32[]{:S(2)}) collective-permute-start(f32[3,2,1,512]{3,2,1,0:T(1,128)S(1)} %pad_maximum_fusion.7), channel_id=1, source_target_pairs={{0,16},{8,24},{16,0},{24,8},{1,17},{9,25},{17,1},{25,9},{2,18},{10... | collective-permute-start | bytes 36872 | tf_op jit(solution)/shard_map/ppermute | solution.py:806
  133.0 36.1 %collective-permute-start.4 = (f32[3,2,1,512]{3,2,1,0:T(1,128)S(1)}, f32[3,2,1,512]{3,2,1,0:T(1,128)S(1)}, u32[]{:S(2)}, u32[]{:S(2)}) collective-permute-start(f32[3,2,1,512]{3,2,1,0:T(1,128)S(1)} %pad_maximum_fusion.7), channel_id=1, source_target_pairs={{0,24},{8,0},{16,8},{24,16},{1,25},{9,1},{17,9},{25,17},{2,26},{10... | collective-permute-start | bytes 36872 | tf_op jit(solution)/shard_map/ppermute | solution.py:806
  135.7 0.9 copy-start
  163.2 20.5 %all-to-all-start.3 = ((f32[4,2,2,16,512]{4,3,2,1,0:T(8,128)}), f32[4,2,2,16,512]{4,3,2,1,0:T(8,128)S(1)}, u32[]{:S(2)}, u32[]{:S(2)}) async-start(f32[4,2,2,16,512]{4,3,2,1,0:T(8,128)} %analysis.1), calls=%async_computation.3 | async-start | bytes 1048576 | tf_op jit(solution)/shard_map/all_to_all | solution.py:820

commit v4 on v3

--- a/solution.py
+++ b/solution.py
@@ -601,10 +601,34 @@
 
 
 def analysis_kernel(
-    back_ref, quad_ref, sign_ref, heat_ref, mag_ref, high_ref, low_ref, out_ref,
-    values, tend, *, step_count,
+    back_ref, quad_ref, sign_ref, heat_ref, mag_ref, high_ref, low_ref, factors_ref,
+    new_heat_ref, new_mag_ref, values, tend, shells, send_sems, recv_sems, *, step_count,
 ):
     step = pl.program_id(0)
+    me = lax.axis_index("row")
+
+    def send(position, shift):
+        return pltpu.make_async_remote_copy(
+            src_ref=shells.at[me, position],
+            dst_ref=shells.at[me, position],
+            send_sem=send_sems.at[shift - 1, position],
+            recv_sem=recv_sems.at[shift - 1, position],
+            device_id={"row": lax.rem(me + shift, step_count)},
+            device_id_type=pl.DeviceIdType.MESH,
+        )
+
+    @pl.when(step == 0)
+    def _():
+        barrier = pltpu.get_barrier_semaphore()
+        for shift in range(1, step_count):
+            pl.semaphore_signal(
+                barrier,
+                inc=1,
+                device_id={"row": lax.rem(me + shift, step_count)},
+                device_id_type=pl.DeviceIdType.MESH,
+            )
+        pl.semaphore_wait(barrier, step_count - 1)
+
     blocks, _, rows, lanes = back_ref.shape
     half = rows // 2
     local = lanes // 2
@@ -659,10 +683,34 @@
                 )
                 for sign in range(2)
             ]
-            out_ref[0, f, c] = ref[c, 0] + time_step * jnp.where(even, parts[0], parts[1])
-
-
-def analysis(back, quad, sign, heat, mag, high, low, step_count):
+            shells[me, step, f, c] = ref[c, 0] + time_step * jnp.where(even, parts[0], parts[1])
+    for shift in range(1, step_count):
+        send(step, shift).start()
+
+    @pl.when(step == step_count - 1)
+    def _():
+        for position in range(step_count):
+            for shift in range(1, step_count):
+                send(position, shift).wait()
+        for f, ref in enumerate((new_heat_ref, new_mag_ref)):
+            for position in range(step_count):
+                for c in range(2):
+                    running = jnp.zeros(shells.shape[-2:], jnp.float32)
+                    scaled = []
+                    for k in range(step_count):
+                        keep = 1.0 - factors_ref[k, 0, f : f + 1]
+                        running = shells[k, position, f, c] + keep * running
+                        scaled.append(running / factors_ref[k, 2, f : f + 1])
+                    running = jnp.zeros_like(running)
+                    mine = running
+                    for k in reversed(range(step_count)):
+                        keep = 1.0 - factors_ref[k, 1, f : f + 1]
+                        running = scaled[k] + keep * running
+                        mine = jnp.where(me == k, running, mine)
+                    ref[c, 0, position * group : (position + 1) * group] = mine
+
+
+def analysis(back, quad, sign, heat, mag, high, low, factors, step_count):
     local, degrees, north = high.shape
     group = local // step_count
     spec = pl.BlockSpec((2, 1, group, degrees), lambda g: (0, 0, g, 0))
@@ -675,21 +723,27 @@
             pl.BlockSpec(quad.shape, lambda g: (0, 0)),
             pl.BlockSpec((group, degrees), lambda g: (g, 0)),
             spec, spec, legendre_spec, legendre_spec,
+            pl.BlockSpec(factors.shape, lambda g: (0, 0, 0, 0)),
         ],
-        out_specs=pl.BlockSpec((1, 2, 2, group, degrees), lambda g: (g, 0, 0, 0, 0)),
-        out_shape=jax.ShapeDtypeStruct((step_count, 2, 2, group, degrees), jnp.float32),
+        out_specs=[pl.BlockSpec(heat.shape, lambda g: (0, 0, 0, 0))] * 2,
+        out_shape=[jax.ShapeDtypeStruct(heat.shape, jnp.float32)] * 2,
         scratch_shapes=[
             pltpu.VMEM((north // 128, local * 8, 128), jnp.float32),
             pltpu.VMEM((degrees // 128, group * 8, 128), jnp.float32),
+            pltpu.VMEM((step_count, step_count, 2, 2, group, degrees), jnp.float32),
+            pltpu.SemaphoreType.DMA((step_count - 1, step_count)),
+            pltpu.SemaphoreType.DMA((step_count - 1, step_count)),
         ],
-        compiler_params=pltpu.CompilerParams(vmem_limit_bytes=VMEM_BYTES),
+        compiler_params=pltpu.CompilerParams(
+            vmem_limit_bytes=VMEM_BYTES, collective_id=0, has_side_effects=True
+        ),
         cost_estimate=pl.CostEstimate(
             flops=2 * 3 * 8 * local * degrees * north,
             bytes_accessed=4 * local * degrees * north,
             transcendentals=0,
         ),
         name="analysis",
-    )(back, quad, sign, heat, mag, high, low)
+    )(back, quad, sign, heat, mag, high, low, factors)
 
 
 def wave_factors(orders, lon_total):
@@ -814,24 +868,10 @@
     back = lax.all_to_all(spectra, "ma", 0, 0, tiled=True)
 
     quad = fejer_weights(north, NLAT)[None, :]
-    right_side = analysis(
-        back, quad, sign, thermal_spectra, induction_potential, high, low, row_count
-    )
-    shells = lax.all_to_all(right_side, "row", 0, 0, tiled=True)
-    spread = lambda k, which: factors[k, which][:, None, None, :]
-    running = jnp.zeros_like(shells[0])
-    scaled = []
-    for k in range(row_count):
-        running = shells[k] + (1.0 - spread(k, 0)) * running
-        scaled.append(running / spread(k, 2))
-    running = jnp.zeros_like(shells[0])
-    solved = []
-    for k in reversed(range(row_count)):
-        running = scaled[k] + (1.0 - spread(k, 1)) * running
-        solved.append(running)
-    solved = lax.all_to_all(jnp.stack(solved[::-1]), "row", 0, 0, tiled=True)
-    solved = jnp.transpose(solved, (1, 2, 0, 3, 4)).reshape(2, 2, 1, local, degrees)
-    return solved[0], solved[1]
+    new_heat, new_mag = analysis(
+        back, quad, sign, thermal_spectra, induction_potential, high, low, factors, row_count
+    )
+    return new_heat, new_mag
 
 
 def program(*args):
@@ -840,6 +880,7 @@
     _, shells, local, degrees = args[1].shape
     fits = (
         shells == 1
+        and row_count > 1
         and (NLAT // 2) % (8 * ma_count) == 0
         and (2 * local) % 128 == 0
         and local % (16 * row_count) == 0

time: 202 us -> 209 us (1.035)
  Pallas kernels: 96.1 us -> 128 us
  blocking collectives: 16.4 us -> 0 us
  waiting for transfers between devices: 37 us -> 30 us
  starting transfers between devices: 32.5 us -> 26.8 us
  local copies, waits for them, and re-layouts: 9.93 us -> 12.7 us
    pallas_call x1, Pallas kernels: 26.6 us -> 58.4 us  [analysis(): pl.pallas_call(functools.partial(analysis_kernel, step_count=step_count),...]
    all_to_all x1 -> x0, blocking collectives: 16.4 us -> none  [kernel_body(): solved = lax.all_to_all(jnp.stack(solved[::-1]), 'row', 0, 0, tiled=True)]
    all_to_all x1 -> x0, waiting for transfers between devices: 14.6 us -> none  [kernel_body(): shells = lax.all_to_all(right_side, 'row', 0, 0, tiled=True)]
    all_to_all x1, waiting for transfers between devices: 2.23 us -> 11 us  [kernel_body(): back = lax.all_to_all(spectra, 'ma', 0, 0, tiled=True)]
    all_to_all x1 -> x0, starting transfers between devices: 5.82 us -> none  [kernel_body(): shells = lax.all_to_all(right_side, 'row', 0, 0, tiled=True)]
    all_to_all x1, waiting for transfers between devices: 10.9 us -> 6.31 us  [kernel_body(): pair = lax.all_to_all(pair, 'ma', 0, 0, tiled=True)]
    ppermute x1, waiting for transfers between devices: 7.96 us -> 12.4 us  [kernel_body(): above = lax.ppermute(pair, 'row', backward)]
    unnamed x14 -> x22, local copies, waits for them, and re-layouts: 2.19 us -> 6.46 us
  transfers between devices with their start and end apart: 9 -> 8, of which waited for: 6 -> 4; matrix products, arithmetic and copies ran while one was open for 6% -> 5% of each run, Pallas kernels for 13% -> 0%
where the time goes in v4:
time: 209 us; the launch traced here: 207 us
  Pallas kernels  128 us (61%)
  waiting for transfers between devices  30 us (14%)
  starting transfers between devices  26.8 us (13%)
  local copies, waits for them, and re-layouts  12.7 us (6%)
  other arithmetic  8.92 us (4%)
    pallas_call x1, Pallas kernels, analysis(): pl.pallas_call(functools.partial(analysis_kernel, step_count=step_count),...  58.4 us
    pallas_call x1, Pallas kernels, synthesis(): pl.pallas_call(functools.partial(synthesis_kernel, step_count=step_count)...  47.4 us
    pallas_call x1, Pallas kernels, grid_step(): pl.pallas_call(functools.partial(grid_kernel, step_count=step_count, slop...  22.1 us
    ppermute x1, waiting for transfers between devices, kernel_body(): above = lax.ppermute(pair, 'row', backward)  12.4 us
    all_to_all x1, waiting for transfers between devices, kernel_body(): back = lax.all_to_all(spectra, 'ma', 0, 0, tiled=True)  11 us
    ppermute x3, starting transfers between devices, kernel_body(): lax.ppermute(small, 'row', [(i, (i + shift) % row_count) for i in range(r...  6.53 us
    unnamed x22, local copies, waits for them, and re-layouts  6.46 us
    all_to_all x1, waiting for transfers between devices, kernel_body(): pair = lax.all_to_all(pair, 'ma', 0, 0, tiled=True)  6.31 us
  transfers between devices with their start and end apart: 8, of which 4 were waited for; matrix products, arithmetic and copies ran while one was open for 5% of the time, Pallas kernels for 0%

profile of v4, /device:TPU:2, one launch (start us, length us, event | category | flops | bytes accessed | tf_op | source)
XLA Modules:
  0.0 207.2 jit_solution(12956712587271378114)
XLA Ops:
  3.7 1.0 fusion.21
  4.7 47.4 %synthesis.1 = (f32[8,2,96,128]{3,2,1,0:T(8,128)}, f32[8,5,96,128]{3,2,1,0:T(8,128)}, bf16[64,512,384]{2,1,0:T(8,128)(2,1)}, bf16[64,512,384]{2,1,0:T(8,128)(2,1)}) custom-call(f32[2,1,64,512]{3,2,1,0:T(8,128)} %psi_ref.1, f32[2,1,64,512]{3,2,1,0:T(8,128)} %heat_ref.3, f32[2,1,64,512]{3,2,1,0:T(8,128)} %mag_ref.3, f32[2,1,64,512]{3,2,1,0:T(8,128)} %speed_ref.1, ...), custom_call_target="tpu_custom_call" | custom-call | flops 3623878656 | bytes 50331648 | tf_op jit(solution)/shard_map/synthesis/pallas_call | solution.py:481
  52.1 4.3 %all-to-all-start = ((f32[8,2,96,128]{3,2,1,0:T(8,128)}), f32[8,2,96,128]{3,2,1,0:T(8,128)S(1)}, u32[]{:S(2)}, u32[]{:S(2)}) async-start(f32[8,2,96,128]{3,2,1,0:T(8,128)} %get-tuple-element.10), calls=%async_computation | async-start | bytes 1572864 | tf_op jit(solution)/shard_map/all_to_all | solution.py:823
  59.0 2.2 %copy.20 = f32[1024,6,4]{2,0,1:T(8,128)} copy(f32[1024,6,4]{0,2,1:T(4,128)S(1)} %reshape.416) | data formatting | bytes 196608 | tf_op jit(solution)/shard_map/reshape | solution.py:836
  61.1 6.3 %all-to-all-done.pair_ref = f32[8,2,96,128]{3,2,1,0:T(8,128)S(1)} async-done(((f32[8,2,96,128]{3,2,1,0:T(8,128)}), f32[8,2,96,128]{3,2,1,0:T(8,128)S(1)}, u32[]{:S(2)}, u32[]{:S(2)}) %all-to-all-start) | async-done | bytes 786464 | tf_op jit(solution)/shard_map/all_to_all | solution.py:823
  67.5 5.0 %all-to-all-start.1 = ((f32[8,5,96,128]{3,2,1,0:T(8,128)}), f32[8,5,96,128]{3,2,1,0:T(8,128)S(1)}, u32[]{:S(2)}, u32[]{:S(2)}) async-start(f32[8,5,96,128]{3,2,1,0:T(8,128)} %get-tuple-element.13), calls=%async_computation.1 | async-start | bytes 3932160 | tf_op jit(solution)/shard_map/all_to_all | solution.py:825
  73.3 2.7 %fusion.6 = f32[384]{0:T(512)S(1)} fusion(f32[384]{0:T(512)S(1)} %fusion.44, s32[384]{0:T(512)S(1)} %get-tuple-element.46, s32[384]{0:T(512)S(1)} %get-tuple-element.47), kind=kLoop, calls=%fused_computation.9 | loop fusion | flops 1621632 | bytes 6144 | tf_op jit(solution)/shard_map/reduce_sum | solution.py:161
  76.6 1.3 collective-permute-start
  77.9 5.5 %collective-permute-start.1 = (f32[8,2,96,128]{3,2,1,0:T(8,128)S(1)}, f32[8,2,96,128]{3,2,1,0:T(8,128)}, u32[]{:S(2)}, u32[]{:S(2)}) collective-permute-start(f32[8,2,96,128]{3,2,1,0:T(8,128)S(1)} %all-to-all-done.pair_ref), channel_id=1, source_target_pairs={{0,8},{8,16},{16,24},{1,9},{9,17},{17,25},{2,10},{10,18},{18,26},{... | collective-permute-start | bytes 2359304 | tf_op jit(solution)/shard_map/ppermute | solution.py:844
  83.4 1.1 fusion.13
  84.7 1.0 pad_maximum_fusion.near_ref
  85.7 12.4 %collective-permute-done.above_ref = f32[8,2,96,128]{3,2,1,0:T(8,128)S(1)} collective-permute-done((f32[8,2,96,128]{3,2,1,0:T(8,128)S(1)}, f32[8,2,96,128]{3,2,1,0:T(8,128)S(1)}, u32[]{:S(2)}, u32[]{:S(2)}) %collective-permute-start) | collective-permute-done | bytes 786464 | tf_op jit(solution)/shard_map/ppermute | solution.py:845
  98.1 0.9 copy-done.8
  99.3 1.3 copy-done.1
  100.5 22.1 %grid_step.1 = f32[8,2,96,128]{3,2,1,0:T(8,128)} custom-call(f32[8,2,96,128]{3,2,1,0:T(8,128)} %copy-done.2, f32[8,5,96,128]{3,2,1,0:T(8,128)} %copy-done.1, f32[8,2,96,128]{3,2,1,0:T(8,128)} %copy-done.8, f32[8,2,96,128]{3,2,1,0:T(8,128)} %collective-permute-done.1.below_ref, f32[1,1024]{1,0:T(1,128)} %reshape.414.weight_ref, f32[1,1024]{1,0:T(1,128)} %reshape.415.spin_ref, ...), custom_call_target="tpu_custom_call" | custom-call | flops 9965666304 | bytes 6291456 | tf_op jit(solution)/shard_map/grid_step/pallas_call | solution.py:578
  122.7 2.6 %collective-permute-start.2 = (f32[3,2,1,512]{3,1,0,2:T(2,128)S(1)}, f32[3,2,1,512]{3,1,0,2:T(2,128)S(1)}, u32[]{:S(2)}, u32[]{:S(2)}) collective-permute-start(f32[3,2,1,512]{3,1,0,2:T(2,128)S(1)} %pad_maximum_fusion.6), channel_id=1, source_target_pairs={{0,8},{8,16},{16,24},{24,0},{1,9},{9,17},{17,25},{25,1},{2,10},{10... | collective-permute-start | bytes 36872 | tf_op jit(solution)/shard_map/ppermute | solution.py:860
  125.3 2.6 %collective-permute-start.3 = (f32[3,2,1,512]{3,1,0,2:T(2,128)S(1)}, f32[3,2,1,512]{3,1,0,2:T(2,128)S(1)}, u32[]{:S(2)}, u32[]{:S(2)}) collective-permute-start(f32[3,2,1,512]{3,1,0,2:T(2,128)S(1)} %pad_maximum_fusion.6), channel_id=1, source_target_pairs={{0,16},{8,24},{16,0},{24,8},{1,17},{9,25},{17,1},{25,9},{2,18},{10... | collective-permute-start | bytes 36872 | tf_op jit(solution)/shard_map/ppermute | solution.py:860
  127.9 1.3 collective-permute-start.4
  129.2 4.2 %all-to-all-start.2 = ((f32[8,2,96,128]{3,2,1,0:T(8,128)}), f32[8,2,96,128]{3,2,1,0:T(8,128)S(1)}, u32[]{:S(2)}, u32[]{:S(2)}) async-start(f32[8,2,96,128]{3,2,1,0:T(8,128)} %grid_step.1), calls=%async_computation.2 | async-start | bytes 1572864 | tf_op jit(solution)/shard_map/all_to_all | solution.py:868
  133.5 11.0 %all-to-all-done.2.back_ref = f32[8,2,96,128]{3,2,1,0:T(8,128)S(1)} async-done(((f32[8,2,96,128]{3,2,1,0:T(8,128)}), f32[8,2,96,128]{3,2,1,0:T(8,128)S(1)}, u32[]{:S(2)}, u32[]{:S(2)}) %all-to-all-start.2) | async-done | bytes 786464 | tf_op jit(solution)/shard_map/all_to_all | solution.py:868
  144.5 0.9 copy-done
  145.4 58.4 %analysis.1 = (f32[2,1,64,512]{3,2,1,0:T(8,128)}, f32[2,1,64,512]{3,2,1,0:T(8,128)}) custom-call(f32[8,2,96,128]{3,2,1,0:T(8,128)} %copy-done, f32[1,384]{1,0:T(1,128)} %mul.373.quad_ref, f32[64,512]{1,0:T(8,128)} %fusion.30.sign_ref, f32[2,1,64,512]{3,2,1,0:T(8,128)} %heat_ref.3, f32[2,1,64,512]{3,2,1,0:T(8,128)} %mag_ref.3, ...), custom_call_target="tpu_custom_call" | custom-call | flops 603979776 | bytes 50331648 | tf_op jit(solution)/shard_map/analysis/pallas_call | solution.py:718
  203.8 1.7 copy.35
  205.5 1.7 copy.36
  (66 shorter events, 7.5 us)
Async XLA Ops:
  4.7 51.6 %copy-start.4 = (s32[512]{0:T(512)S(1)}, s32[512]{0:T(512)}, u32[]{:S(2)}) copy-start(s32[512]{0:T(512)} %param.12) | copy-start | bytes 6148
  4.7 51.8 %copy-start.5 = (f32[2,1,512]{2,1,0:T(1,128)S(1)}, f32[2,1,512]{2,1,0:T(1,128)}, u32[]{:S(2)}) copy-start(f32[2,1,512]{2,1,0:T(1,128)} %param.13) | copy-start | bytes 12292
  52.1 15.4 %all-to-all-start = ((f32[8,2,96,128]{3,2,1,0:T(8,128)}), f32[8,2,96,128]{3,2,1,0:T(8,128)S(1)}, u32[]{:S(2)}, u32[]{:S(2)}) async-start(f32[8,2,96,128]{3,2,1,0:T(8,128)} %get-tuple-element.10), calls=%async_computation | async-start | bytes 1572864 | tf_op jit(solution)/shard_map/all_to_all | solution.py:823
  58.9 24.4 %copy-start.6 = (f32[2,1,512]{2,1,0:T(1,128)S(1)}, f32[2,1,512]{2,1,0:T(1,128)}, u32[]{:S(2)}) copy-start(f32[2,1,512]{2,1,0:T(1,128)} %param.15) | copy-start | bytes 12292
  58.9 24.4 %copy-start.7 = (f32[2,1,512]{2,1,0:T(1,128)S(1)}, f32[2,1,512]{2,1,0:T(1,128)}, u32[]{:S(2)}) copy-start(f32[2,1,512]{2,1,0:T(1,128)} %param.14) | copy-start | bytes 12292
  67.5 17.2 %copy-start.2 = (f32[8,2,96,128]{3,2,1,0:T(8,128)}, f32[8,2,96,128]{3,2,1,0:T(8,128)S(1)}, u32[]{:S(2)}) copy-start(f32[8,2,96,128]{3,2,1,0:T(8,128)S(1)} %all-to-all-done.pair_ref) | copy-start | bytes 2359300
  67.5 31.8 %all-to-all-start.1 = ((f32[8,5,96,128]{3,2,1,0:T(8,128)}), f32[8,5,96,128]{3,2,1,0:T(8,128)S(1)}, u32[]{:S(2)}, u32[]{:S(2)}) async-start(f32[8,5,96,128]{3,2,1,0:T(8,128)} %get-tuple-element.13), calls=%async_computation.1 | async-start | bytes 3932160 | tf_op jit(solution)/shard_map/all_to_all | solution.py:825
  76.6 21.5 %collective-permute-start = (f32[8,2,96,128]{3,2,1,0:T(8,128)S(1)}, f32[8,2,96,128]{3,2,1,0:T(8,128)S(1)}, u32[]{:S(2)}, u32[]{:S(2)}) collective-permute-start(f32[8,2,96,128]{3,2,1,0:T(8,128)S(1)} %all-to-all-done.pair_ref), channel_id=1, source_target_pairs={{8,0},{16,8},{24,16},{9,1},{17,9},{25,17},{10,2},{18,10},{26,18},{... | collective-permute-start | bytes 2359304 | tf_op jit(solution)/shard_map/ppermute | solution.py:845
  77.9 21.4 %collective-permute-start.1 = (f32[8,2,96,128]{3,2,1,0:T(8,128)S(1)}, f32[8,2,96,128]{3,2,1,0:T(8,128)}, u32[]{:S(2)}, u32[]{:S(2)}) collective-permute-start(f32[8,2,96,128]{3,2,1,0:T(8,128)S(1)} %all-to-all-done.pair_ref), channel_id=1, source_target_pairs={{0,8},{8,16},{16,24},{1,9},{9,17},{17,25},{2,10},{10,18},{18,26},{... | collective-permute-start | bytes 2359304 | tf_op jit(solution)/shard_map/ppermute | solution.py:844
  98.1 0.9 copy-start.8
  99.3 1.3 copy-start.1
  122.7 10.8 %collective-permute-start.2 = (f32[3,2,1,512]{3,1,0,2:T(2,128)S(1)}, f32[3,2,1,512]{3,1,0,2:T(2,128)S(1)}, u32[]{:S(2)}, u32[]{:S(2)}) collective-permute-start(f32[3,2,1,512]{3,1,0,2:T(2,128)S(1)} %pad_maximum_fusion.6), channel_id=1, source_target_pairs={{0,8},{8,16},{16,24},{24,0},{1,9},{9,17},{17,25},{25,1},{2,10},{10... | collective-permute-start | bytes 36872 | tf_op jit(solution)/shard_map/ppermute | solution.py:860
  125.3 8.2 %collective-permute-start.3 = (f32[3,2,1,512]{3,1,0,2:T(2,128)S(1)}, f32[3,2,1,512]{3,1,0,2:T(2,128)S(1)}, u32[]{:S(2)}, u32[]{:S(2)}) collective-permute-start(f32[3,2,1,512]{3,1,0,2:T(2,128)S(1)} %pad_maximum_fusion.6), channel_id=1, source_target_pairs={{0,16},{8,24},{16,0},{24,8},{1,17},{9,25},{17,1},{25,9},{2,18},{10... | collective-permute-start | bytes 36872 | tf_op jit(solution)/shard_map/ppermute | solution.py:860
  127.9 5.6 %collective-permute-start.4 = (f32[3,2,1,512]{3,1,0,2:T(2,128)S(1)}, f32[3,2,1,512]{3,1,0,2:T(2,128)S(1)}, u32[]{:S(2)}, u32[]{:S(2)}) collective-permute-start(f32[3,2,1,512]{3,1,0,2:T(2,128)S(1)} %pad_maximum_fusion.6), channel_id=1, source_target_pairs={{0,24},{8,0},{16,8},{24,16},{1,25},{9,1},{17,9},{25,17},{2,26},{10... | collective-permute-start | bytes 36872 | tf_op jit(solution)/shard_map/ppermute | solution.py:860
  129.2 15.3 %all-to-all-start.2 = ((f32[8,2,96,128]{3,2,1,0:T(8,128)}), f32[8,2,96,128]{3,2,1,0:T(8,128)S(1)}, u32[]{:S(2)}, u32[]{:S(2)}) async-start(f32[8,2,96,128]{3,2,1,0:T(8,128)} %grid_step.1), calls=%async_computation.2 | async-start | bytes 1572864 | tf_op jit(solution)/shard_map/all_to_all | solution.py:868
  133.5 11.0 %copy-start.3 = (f32[4,3,2,512]{3,2,1,0:T(2,128)}, f32[4,3,2,512]{3,2,1,0:T(2,128)S(1)}, u32[]{:S(2)}) copy-start(f32[4,3,2,512]{3,2,1,0:T(2,128)S(1)} %bitcast_dynamic-update-slice_fusion.factors_ref) | copy-start | bytes 147460
  144.5 0.9 copy-start
